TPU v7x, 32 devices: a whole 2x2x4 slice. The times are simulated.
32 devices in a mesh: gx: 4 (over y, x), gy: 2 (over core), gz: 4 (over z).
Axes of the slice: x: 2, y: 2, z: 4, core: 2. Of those that a mesh axis runs over, the one named last changes fastest.
Arguments:
- press_prev: float32 [64, 64, 512], P('gx', 'gy', 'gz'), may hold values from -6 to 6
- press_now: float32 [64, 64, 512], P('gx', 'gy', 'gz'), may hold values from -6 to 6
- board_prev: float32 [64, 64], P('gx', 'gy'), may hold values from -6 to 6
- board_now: float32 [64, 64], P('gx', 'gy'), may hold values from -6 to 6
- costate_prev: float32 [64, 64, 512], P('gx', 'gy', 'gz'), may hold values from -6 to 6
- costate_now: float32 [64, 64, 512], P('gx', 'gy', 'gz'), may hold values from -6 to 6
- adjoint_prev: float32 [64, 64], P('gx', 'gy'), may hold values from -6 to 6
- adjoint_now: float32 [64, 64], P('gx', 'gy'), may hold values from -6 to 6
- speed: float32 [64, 64, 512], P('gx', 'gy', 'gz'), may hold values from 0.12 to 0.32
- stiffness: float32 [64, 64], P('gx', 'gy'), may hold values from 0.4 to 1.6
- plate_mask: int32 [64, 64], P('gx', 'gy'), may hold values 0 or 1
- height: int32 [64, 64], P('gx', 'gy'), may hold values from 193 to 318
- source_cells: int32 [88], replicated, may hold values from 0 to 4095
- source_force: float32 [4, 88], replicated, may hold values from -12 to 12
Outputs:
- costate_first: float32 [64, 64, 512], P('gx', 'gy', 'gz')
- costate_second: float32 [64, 64, 512], P('gx', 'gy', 'gz')
- adjoint_first: float32 [64, 64], P('gx', 'gy')
- adjoint_second: float32 [64, 64], P('gx', 'gy')
- stiffness_grad: float32 [64, 64], P('gx', 'gy')
Inputs may be any that keep to these rules, and one draw needn't show every extreme that they name: Every plate cell sits within 64 cells of the middle of the height. `source_cells`: flat indices of plate cells; points may repeat and may lie off the soundboard.
All inputs are finite; a program needn't handle non-finite values. No bound on the sum of `plate_mask` on one device may be relied on, other than what follows from the above.
Results may differ from a plain program's by a relative error of at most 0.022.
Values sent between devices are 32-bit elements; how exact they have to be, the bound alone decides.
A program may use at most 128 MiB of HBM per device.

v0:
```python
import jax
import jax.numpy as jnp
from jax import lax
from jax.sharding import PartitionSpec as P

STEPS = 4


DRIVE_GAIN = 0.5
LOAD_GAIN = 0.5
BEND_GAIN = 0.035


def padded_2(cells, sides, width):
    for axis, dim in sides:
        count = lax.axis_size(axis)
        ends = count - 1
        head = lax.slice_in_dim(cells, 0, width, axis=dim)
        tail = lax.slice_in_dim(cells, cells.shape[dim] - width, cells.shape[dim], axis=dim)
        cells = jnp.concatenate(
            [
                lax.ppermute(tail, axis, [(i, (i + 1) % count) for i in range(ends)]),
                cells,
                lax.ppermute(head, axis, [((i + 1) % count, i) for i in range(ends)]),
            ],
            axis=dim,
        )
    return cells


def lap_cube(padded):
    total = padded[2:, 1:-1, 1:-1] + padded[:-2, 1:-1, 1:-1]
    total = total + padded[1:-1, 2:, 1:-1] + padded[1:-1, :-2, 1:-1]
    total = total + padded[1:-1, 1:-1, 2:] + padded[1:-1, 1:-1, :-2]
    return total - 6.0 * padded[1:-1, 1:-1, 1:-1]


def lap_sheet(padded):
    total = padded[2:, 1:-1] + padded[:-2, 1:-1] + padded[1:-1, 2:] + padded[1:-1, :-2]
    return total - 4.0 * padded[1:-1, 1:-1]


def on_device(
    press_prev,
    press_now,
    board_prev,
    board_now,
    costate_prev,
    costate_now,
    adjoint_prev,
    adjoint_now,
    speed,
    stiffness,
    plate_mask,
    height,
    source_cells,
    source_force,
):
    cells_x, cells_y, cells_z = press_now.shape
    rows_y = cells_y * lax.axis_size("gy")
    mask_f = plate_mask.astype(jnp.float32)
    anchor_x = lax.axis_index("gx") * cells_x
    anchor_y = lax.axis_index("gy") * cells_y
    anchor_z = lax.axis_index("gz") * cells_z
    level_z = anchor_z + jnp.arange(cells_z, dtype=jnp.int32)
    dipole = (level_z[None, None, :] == (height + 1)[:, :, None]).astype(jnp.float32) - (
        level_z[None, None, :] == (height - 1)[:, :, None]
    ).astype(jnp.float32)
    xpos = source_cells // rows_y
    ypos = source_cells % rows_y
    hit_x = (xpos[:, None] == anchor_x + jnp.arange(cells_x, dtype=jnp.int32)[None, :]).astype(
        jnp.float32
    )
    hit_y = (ypos[:, None] == anchor_y + jnp.arange(cells_y, dtype=jnp.int32)[None, :]).astype(
        jnp.float32
    )
    forcing = jnp.einsum(
        "ts,sx,sy->txy", source_force, hit_x, hit_y, precision=lax.Precision.HIGHEST
    )

    def bending(field):
        curve = lap_sheet(padded_2(field, (("gx", 0), ("gy", 1)), 1))
        weighted = padded_2(stiffness * curve, (("gx", 0), ("gy", 1)), 1)
        return (curve, lap_sheet(weighted))

    board_prev = mask_f * board_prev
    board_now = mask_f * board_now
    curves = []
    backs = {}
    for counter in range(STEPS):
        padded = padded_2(press_now, (("gx", 0), ("gy", 1), ("gz", 2)), 1)
        press_next = (
            2.0 * press_now
            - press_prev
            + speed * lap_cube(padded)
            + DRIVE_GAIN * (board_now - board_prev)[:, :, None] * dipole
        )
        plate_curve, bent = bending(board_now)
        board_next = mask_f * (
            2.0 * board_now
            - board_prev
            - BEND_GAIN * bent
            + LOAD_GAIN * lax.psum(-jnp.sum(press_now * dipole, axis=2), "gz")
            + forcing[counter]
        )
        board_next, curve = (board_next, plate_curve)
        curves.append(curve)
        press_prev, press_now = (press_now, press_next)
        board_prev, board_now = (board_now, board_next)
    for counter in reversed(range(STEPS)):
        react = DRIVE_GAIN * lax.psum(jnp.sum(costate_now * dipole, axis=2), "gz")
        padded = padded_2(speed * costate_now, (("gx", 0), ("gy", 1), ("gz", 2)), 1)
        masked = mask_f * adjoint_now
        curve_back, bent_back = bending(masked)
        costate_next = (
            costate_prev
            + 2.0 * costate_now
            + lap_cube(padded)
            - LOAD_GAIN * masked[:, :, None] * dipole
        )
        adjoint_next = adjoint_prev + 2.0 * masked - BEND_GAIN * bent_back + react
        costate_prev, costate_now, adjoint_prev, adjoint_now, curve_back = (
            -costate_now,
            costate_next,
            -masked - react,
            adjoint_next,
            curve_back,
        )
        backs[counter] = curve_back
    gradient = jnp.zeros_like(stiffness)
    for counter in reversed(range(STEPS)):
        gradient = gradient - BEND_GAIN * curves[counter] * backs[counter]
    return (costate_prev, costate_now, adjoint_prev, adjoint_now, gradient)


def solution(mesh):
    return jax.shard_map(
        on_device,
        mesh=mesh,
        in_specs=(
            P("gx", "gy", "gz"),
            P("gx", "gy", "gz"),
            P("gx", "gy"),
            P("gx", "gy"),
            P("gx", "gy", "gz"),
            P("gx", "gy", "gz"),
            P("gx", "gy"),
            P("gx", "gy"),
            P("gx", "gy", "gz"),
            P("gx", "gy"),
            P("gx", "gy"),
            P("gx", "gy"),
            P(),
            P(),
        ),
        out_specs=(
            P("gx", "gy", "gz"),
            P("gx", "gy", "gz"),
            P("gx", "gy"),
            P("gx", "gy"),
            P("gx", "gy"),
        ),
        check_vma=False,
    )
```

profile of v0, /device:TPU:0, one launch (start us, length us, event | category | flops | bytes accessed | tf_op | source)
XLA Modules:
  0.0 349.6 jit_solution(5971545915376587483)
XLA Ops:
  3.1 5.6 %collective-permute-start.1 = (f32[1,32,128]{2,1,0:T(8,128)S(1)}, f32[1,32,128]{2,1,0:T(8,128)S(1)}, u32[]{:S(2)}, u32[]{:S(2)}) collective-permute-start(f32[1,32,128]{2,1,0:T(8,128)S(1)} %get-tuple-element.83), channel_id=1, source_target_pairs={{0,8},{8,16},{16,24},{1,9},{9,17},{17,25},{2,10},{10,18},{18,26},{... | collective-permute-start | bytes 49160 | tf_op jit(solution)/shard_map/ppermute | solution.py:22
  8.7 4.8 %collective-permute-start.73 = (f32[1,32,128]{2,1,0:T(8,128)S(1)}, f32[1,32,128]{2,1,0:T(8,128)S(1)}, u32[]{:S(2)}, u32[]{:S(2)}) collective-permute-start(f32[1,32,128]{2,1,0:T(8,128)S(1)} %get-tuple-element.86), channel_id=1, source_target_pairs={{0,8},{8,16},{16,24},{1,9},{9,17},{17,25},{2,10},{10,18},{18,26},{... | collective-permute-start | bytes 49160 | tf_op jit(solution)/shard_map/ppermute | solution.py:22
  15.0 4.5 %collective-permute-start.13 = (f32[1,32]{1,0:T(1,128)S(1)}, f32[1,32]{1,0:T(1,128)S(1)}, u32[]{:S(2)}, u32[]{:S(2)}) collective-permute-start(f32[1,32]{1,0:T(1,128)S(1)} %get-tuple-element.147), channel_id=1, source_target_pairs={{0,8},{8,16},{16,24},{1,9},{9,17},{17,25},{2,10},{10,18},{18,26},{... | collective-permute-start | bytes 392 | tf_op jit(solution)/shard_map/ppermute | solution.py:22
  22.6 4.5 %collective-permute-start.57 = (f32[1,32]{1,0:T(1,128)S(1)}, f32[1,32]{1,0:T(1,128)S(1)}, u32[]{:S(2)}, u32[]{:S(2)}) collective-permute-start(f32[1,32]{1,0:T(1,128)S(1)} %get-tuple-element.139), channel_id=1, source_target_pairs={{0,8},{8,16},{16,24},{1,9},{9,17},{17,25},{2,10},{10,18},{18,26},{... | collective-permute-start | bytes 392 | tf_op jit(solution)/shard_map/ppermute | solution.py:22
  37.4 4.9 %collective-permute-start.17 = (f32[1,32]{1,0:T(1,128)S(1)}, f32[1,32]{1,0:T(1,128)S(1)}, u32[]{:S(2)}, u32[]{:S(2)}) collective-permute-start(f32[1,32]{1,0:T(1,128)S(1)} %get-tuple-element.145), channel_id=1, source_target_pairs={{0,8},{8,16},{16,24},{1,9},{9,17},{17,25},{2,10},{10,18},{18,26},{... | collective-permute-start | bytes 392 | tf_op jit(solution)/shard_map/ppermute | solution.py:22
  43.8 5.4 %collective-permute-start.61 = (f32[1,32]{1,0:T(1,128)S(1)}, f32[1,32]{1,0:T(1,128)S(1)}, u32[]{:S(2)}, u32[]{:S(2)}) collective-permute-start(f32[1,32]{1,0:T(1,128)S(1)} %get-tuple-element.137), channel_id=1, source_target_pairs={{0,8},{8,16},{16,24},{1,9},{9,17},{17,25},{2,10},{10,18},{18,26},{... | collective-permute-start | bytes 392 | tf_op jit(solution)/shard_map/ppermute | solution.py:22
  62.3 4.6 %collective-permute-start.5 = (f32[18,34,1]{2,1,0:T(8,128)S(1)}, f32[18,34,1]{2,1,0:T(8,128)S(1)}, u32[]{:S(2)}, u32[]{:S(2)}) collective-permute-start(f32[18,34,1]{2,1,0:T(8,128)S(1)} %get-tuple-element.58), channel_id=1, source_target_pairs={{0,1},{1,2},{2,3},{4,5},{5,6},{6,7},{8,9},{9,10},{10,11},{12,13},{... | collective-permute-start | bytes 7352 | tf_op jit(solution)/shard_map/ppermute | solution.py:22
  68.6 4.6 %collective-permute-start.77 = (f32[18,34,1]{2,1,0:T(8,128)S(1)}, f32[18,34,1]{2,1,0:T(8,128)S(1)}, u32[]{:S(2)}, u32[]{:S(2)}) collective-permute-start(f32[18,34,1]{2,1,0:T(8,128)S(1)} %get-tuple-element.60), channel_id=1, source_target_pairs={{0,1},{1,2},{2,3},{4,5},{5,6},{6,7},{8,9},{9,10},{10,11},{12,13},{... | collective-permute-start | bytes 7352 | tf_op jit(solution)/shard_map/ppermute | solution.py:22
  83.9 20.0 %all-reduce.1 = (f32[16,32]{1,0:T(8,128)S(1)}, f32[16,32]{1,0:T(8,128)S(1)}, f32[16,32]{1,0:T(8,128)S(1)}) all-reduce(f32[16,32]{1,0:T(8,128)S(1)} %get-tuple-element.6, f32[16,32]{1,0:T(8,128)S(1)} %get-tuple-element.7, f32[16,32]{1,0:T(8,128)S(1)} %neg.41), channel_id=1, replica_groups=mesh['gx'=4,'gy'=2,'gz'=4] {'gz'}, use_global_device_ids=true, to_apply=%region_1.2 | all-reduce | flops 1536 | bytes 12288 | tf_op jit(solution)/shard_map/psum | solution.py:111
  105.3 6.1 %collective-permute-start.27 = (f32[1,32]{1,0:T(1,128)S(1)}, f32[1,32]{1,0:T(1,128)S(1)}, u32[]{:S(2)}, u32[]{:S(2)}) collective-permute-start(f32[1,32]{1,0:T(1,128)S(1)} %get-tuple-element.143), channel_id=1, source_target_pairs={{0,8},{8,16},{16,24},{1,9},{9,17},{17,25},{2,10},{10,18},{18,26},{... | collective-permute-start | bytes 392 | tf_op jit(solution)/shard_map/ppermute | solution.py:22
  112.8 5.5 %collective-permute-start.87 = (f32[1,32,128]{2,1,0:T(8,128)S(1)}, f32[1,32,128]{2,1,0:T(8,128)S(1)}, u32[]{:S(2)}, u32[]{:S(2)}) collective-permute-start(f32[1,32,128]{2,1,0:T(8,128)S(1)} %get-tuple-element.73), channel_id=1, source_target_pairs={{0,8},{8,16},{16,24},{1,9},{9,17},{17,25},{2,10},{10,18},{18,26},{... | collective-permute-start | bytes 49160 | tf_op jit(solution)/shard_map/ppermute | solution.py:22
  121.0 6.1 %collective-permute-start.65 = (f32[1,32]{1,0:T(1,128)S(1)}, f32[1,32]{1,0:T(1,128)S(1)}, u32[]{:S(2)}, u32[]{:S(2)}) collective-permute-start(f32[1,32]{1,0:T(1,128)S(1)} %get-tuple-element.131), channel_id=1, source_target_pairs={{0,8},{8,16},{16,24},{1,9},{9,17},{17,25},{2,10},{10,18},{18,26},{... | collective-permute-start | bytes 392 | tf_op jit(solution)/shard_map/ppermute | solution.py:22
  137.3 5.4 %collective-permute-start.31 = (f32[1,32]{1,0:T(1,128)S(1)}, f32[1,32]{1,0:T(1,128)S(1)}, u32[]{:S(2)}, u32[]{:S(2)}) collective-permute-start(f32[1,32]{1,0:T(1,128)S(1)} %get-tuple-element.141), channel_id=1, source_target_pairs={{0,8},{8,16},{16,24},{1,9},{9,17},{17,25},{2,10},{10,18},{18,26},{... | collective-permute-start | bytes 392 | tf_op jit(solution)/shard_map/ppermute | solution.py:22
  144.2 5.4 %collective-permute-start.69 = (f32[1,32]{1,0:T(1,128)S(1)}, f32[1,32]{1,0:T(1,128)S(1)}, u32[]{:S(2)}, u32[]{:S(2)}) collective-permute-start(f32[1,32]{1,0:T(1,128)S(1)} %get-tuple-element.129), channel_id=1, source_target_pairs={{0,8},{8,16},{16,24},{1,9},{9,17},{17,25},{2,10},{10,18},{18,26},{... | collective-permute-start | bytes 392 | tf_op jit(solution)/shard_map/ppermute | solution.py:22
  156.3 5.4 %collective-permute-start.41 = (f32[1,32]{1,0:T(1,128)S(1)}, f32[1,32]{1,0:T(1,128)S(1)}, u32[]{:S(2)}, u32[]{:S(2)}) collective-permute-start(f32[1,32]{1,0:T(1,128)S(1)} %get-tuple-element.135), channel_id=1, source_target_pairs={{0,8},{8,16},{16,24},{1,9},{9,17},{17,25},{2,10},{10,18},{18,26},{... | collective-permute-start | bytes 392 | tf_op jit(solution)/shard_map/ppermute | solution.py:22
  169.7 5.4 %collective-permute-start.45 = (f32[1,32]{1,0:T(1,128)S(1)}, f32[1,32]{1,0:T(1,128)S(1)}, u32[]{:S(2)}, u32[]{:S(2)}) collective-permute-start(f32[1,32]{1,0:T(1,128)S(1)} %get-tuple-element.133), channel_id=1, source_target_pairs={{0,8},{8,16},{16,24},{1,9},{9,17},{17,25},{2,10},{10,18},{18,26},{... | collective-permute-start | bytes 392 | tf_op jit(solution)/shard_map/ppermute | solution.py:22
  175.1 5.1 %collective-permute-start.7 = (f32[1,32,128]{2,1,0:T(8,128)S(1)}, f32[1,32,128]{2,1,0:T(8,128)S(1)}, u32[]{:S(2)}, u32[]{:S(2)}) collective-permute-start(f32[1,32,128]{2,1,0:T(8,128)S(1)} %get-tuple-element.81), channel_id=1, source_target_pairs={{0,8},{8,16},{16,24},{1,9},{9,17},{17,25},{2,10},{10,18},{18,26},{... | collective-permute-start | bytes 49160 | tf_op jit(solution)/shard_map/ppermute | solution.py:22
  190.2 4.6 %collective-permute-start.11 = (f32[18,34,1]{2,1,0:T(8,128)S(1)}, f32[18,34,1]{2,1,0:T(8,128)S(1)}, u32[]{:S(2)}, u32[]{:S(2)}) collective-permute-start(f32[18,34,1]{2,1,0:T(8,128)S(1)} %get-tuple-element.56), channel_id=1, source_target_pairs={{0,1},{1,2},{2,3},{4,5},{5,6},{6,7},{8,9},{9,10},{10,11},{12,13},{... | collective-permute-start | bytes 7352 | tf_op jit(solution)/shard_map/ppermute | solution.py:22
  194.8 7.3 %collective-permute-done.10 = f32[18,34,1]{2,1,0:T(8,128)S(1)} collective-permute-done((f32[18,34,1]{2,1,0:T(8,128)S(1)}, f32[18,34,1]{2,1,0:T(8,128)S(1)}, u32[]{:S(2)}, u32[]{:S(2)}) %collective-permute-start.10) | collective-permute-done | bytes 2480 | tf_op jit(solution)/shard_map/ppermute | solution.py:24
  208.3 4.8 %collective-permute-start.21 = (f32[1,32,128]{2,1,0:T(8,128)S(1)}, f32[1,32,128]{2,1,0:T(8,128)S(1)}, u32[]{:S(2)}, u32[]{:S(2)}) collective-permute-start(f32[1,32,128]{2,1,0:T(8,128)S(1)} %get-tuple-element.79), channel_id=1, source_target_pairs={{0,8},{8,16},{16,24},{1,9},{9,17},{17,25},{2,10},{10,18},{18,26},{... | collective-permute-start | bytes 49160 | tf_op jit(solution)/shard_map/ppermute | solution.py:22
  220.4 4.6 %collective-permute-start.91 = (f32[18,34,1]{2,1,0:T(8,128)S(1)}, f32[18,34,1]{2,1,0:T(8,128)S(1)}, u32[]{:S(2)}, u32[]{:S(2)}) collective-permute-start(f32[18,34,1]{2,1,0:T(8,128)S(1)} %get-tuple-element.50), channel_id=1, source_target_pairs={{0,1},{1,2},{2,3},{4,5},{5,6},{6,7},{8,9},{9,10},{10,11},{12,13},{... | collective-permute-start | bytes 7352 | tf_op jit(solution)/shard_map/ppermute | solution.py:22
  225.2 5.7 %collective-permute-done.90 = f32[18,34,1]{2,1,0:T(8,128)S(1)} collective-permute-done((f32[18,34,1]{2,1,0:T(8,128)S(1)}, f32[18,34,1]{2,1,0:T(8,128)S(1)}, u32[]{:S(2)}, u32[]{:S(2)}) %collective-permute-start.90) | collective-permute-done | bytes 2480 | tf_op jit(solution)/shard_map/ppermute | solution.py:24
  232.2 4.6 %collective-permute-start.25 = (f32[18,34,1]{2,1,0:T(8,128)S(1)}, f32[18,34,1]{2,1,0:T(8,128)S(1)}, u32[]{:S(2)}, u32[]{:S(2)}) collective-permute-start(f32[18,34,1]{2,1,0:T(8,128)S(1)} %get-tuple-element.54), channel_id=1, source_target_pairs={{0,1},{1,2},{2,3},{4,5},{5,6},{6,7},{8,9},{9,10},{10,11},{12,13},{... | collective-permute-start | bytes 7352 | tf_op jit(solution)/shard_map/ppermute | solution.py:22
  243.7 18.7 %all-reduce = (f32[16,32]{1,0:T(8,128)S(1)}, f32[16,32]{1,0:T(8,128)S(1)}, f32[16,32]{1,0:T(8,128)S(1)}, f32[16,32]{1,0:T(8,128)S(1)}) all-reduce(f32[16,32]{1,0:T(8,128)S(1)} %get-tuple-element.10, f32[16,32]{1,0:T(8,128)S(1)} %get-tuple-element.9, f32[16,32]{1,0:T(8,128)S(1)} %neg.42, ...), channel_id=1, replica_groups=mesh['gx'=4,'gy'=2,'gz'=4] {'gz'}, use_global_device_ids=true, to_apply=%region_5.6 | all-reduce | flops 2048 | bytes 16384 | tf_op jit(solution)/shard_map/psum | solution.py:111
  264.5 5.4 %collective-permute-start.49 = (f32[1,32]{1,0:T(1,128)S(1)}, f32[1,32]{1,0:T(1,128)S(1)}, u32[]{:S(2)}, u32[]{:S(2)}) collective-permute-start(f32[1,32]{1,0:T(1,128)S(1)} %get-tuple-element.121), channel_id=1, source_target_pairs={{0,8},{8,16},{16,24},{1,9},{9,17},{17,25},{2,10},{10,18},{18,26},{... | collective-permute-start | bytes 392 | tf_op jit(solution)/shard_map/ppermute | solution.py:22
  271.3 5.7 %collective-permute-start.79 = (f32[1,32]{1,0:T(1,128)S(1)}, f32[1,32]{1,0:T(1,128)S(1)}, u32[]{:S(2)}, u32[]{:S(2)}) collective-permute-start(f32[1,32]{1,0:T(1,128)S(1)} %get-tuple-element.127), channel_id=1, source_target_pairs={{0,8},{8,16},{16,24},{1,9},{9,17},{17,25},{2,10},{10,18},{18,26},{... | collective-permute-start | bytes 392 | tf_op jit(solution)/shard_map/ppermute | solution.py:22
  285.8 6.1 %collective-permute-start.83 = (f32[1,32]{1,0:T(1,128)S(1)}, f32[1,32]{1,0:T(1,128)S(1)}, u32[]{:S(2)}, u32[]{:S(2)}) collective-permute-start(f32[1,32]{1,0:T(1,128)S(1)} %get-tuple-element.125), channel_id=1, source_target_pairs={{0,8},{8,16},{16,24},{1,9},{9,17},{17,25},{2,10},{10,18},{18,26},{... | collective-permute-start | bytes 392 | tf_op jit(solution)/shard_map/ppermute | solution.py:22
  299.9 5.4 %collective-permute-start.93 = (f32[1,32]{1,0:T(1,128)S(1)}, f32[1,32]{1,0:T(1,128)S(1)}, u32[]{:S(2)}, u32[]{:S(2)}) collective-permute-start(f32[1,32]{1,0:T(1,128)S(1)} %get-tuple-element.123), channel_id=1, source_target_pairs={{0,8},{8,16},{16,24},{1,9},{9,17},{17,25},{2,10},{10,18},{18,26},{... | collective-permute-start | bytes 392 | tf_op jit(solution)/shard_map/ppermute | solution.py:22
  314.5 5.6 %collective-permute-start.53 = (f32[1,32]{1,0:T(1,128)S(1)}, f32[1,32]{1,0:T(1,128)S(1)}, u32[]{:S(2)}, u32[]{:S(2)}) collective-permute-start(f32[1,32]{1,0:T(1,128)S(1)} %get-tuple-element.119), channel_id=1, source_target_pairs={{0,8},{8,16},{16,24},{1,9},{9,17},{17,25},{2,10},{10,18},{18,26},{... | collective-permute-start | bytes 392 | tf_op jit(solution)/shard_map/ppermute | solution.py:22
  320.2 4.8 %collective-permute-start.35 = (f32[1,32,128]{2,1,0:T(8,128)S(1)}, f32[1,32,128]{2,1,0:T(8,128)S(1)}, u32[]{:S(2)}, u32[]{:S(2)}) collective-permute-start(f32[1,32,128]{2,1,0:T(8,128)S(1)} %get-tuple-element.75), channel_id=1, source_target_pairs={{0,8},{8,16},{16,24},{1,9},{9,17},{17,25},{2,10},{10,18},{18,26},{... | collective-permute-start | bytes 49160 | tf_op jit(solution)/shard_map/ppermute | solution.py:22
  336.7 4.6 %collective-permute-start.39 = (f32[18,34,1]{2,1,0:T(8,128)S(1)}, f32[18,34,1]{2,1,0:T(8,128)S(1)}, u32[]{:S(2)}, u32[]{:S(2)}) collective-permute-start(f32[18,34,1]{2,1,0:T(8,128)S(1)} %get-tuple-element.52), channel_id=1, source_target_pairs={{0,1},{1,2},{2,3},{4,5},{5,6},{6,7},{8,9},{9,10},{10,11},{12,13},{... | collective-permute-start | bytes 7352 | tf_op jit(solution)/shard_map/ppermute | solution.py:22
  342.0 5.2 %collective-permute-done.38 = f32[18,34,1]{2,1,0:T(8,128)S(1)} collective-permute-done((f32[18,34,1]{2,1,0:T(8,128)S(1)}, f32[18,34,1]{2,1,0:T(8,128)S(1)}, u32[]{:S(2)}, u32[]{:S(2)}) %collective-permute-start.38) | collective-permute-done | bytes 2480 | tf_op jit(solution)/shard_map/ppermute | solution.py:24
  (296 shorter events, 150.5 us)
Async XLA Ops:
  1.8 50.2 %collective-permute-start = (f32[1,32,128]{2,1,0:T(8,128)S(1)}, f32[1,32,128]{2,1,0:T(8,128)S(1)}, u32[]{:S(2)}, u32[]{:S(2)}) collective-permute-start(f32[1,32,128]{2,1,0:T(8,128)S(1)} %get-tuple-element.84), channel_id=1, source_target_pairs={{8,0},{16,8},{24,16},{9,1},{17,9},{25,17},{10,2},{18,10},{26,18},{... | collective-permute-start | bytes 49160 | tf_op jit(solution)/shard_map/ppermute | solution.py:24
  3.1 48.8 %collective-permute-start.1 = (f32[1,32,128]{2,1,0:T(8,128)S(1)}, f32[1,32,128]{2,1,0:T(8,128)S(1)}, u32[]{:S(2)}, u32[]{:S(2)}) collective-permute-start(f32[1,32,128]{2,1,0:T(8,128)S(1)} %get-tuple-element.83), channel_id=1, source_target_pairs={{0,8},{8,16},{16,24},{1,9},{9,17},{17,25},{2,10},{10,18},{18,26},{... | collective-permute-start | bytes 49160 | tf_op jit(solution)/shard_map/ppermute | solution.py:22
  8.7 47.6 %collective-permute-start.73 = (f32[1,32,128]{2,1,0:T(8,128)S(1)}, f32[1,32,128]{2,1,0:T(8,128)S(1)}, u32[]{:S(2)}, u32[]{:S(2)}) collective-permute-start(f32[1,32,128]{2,1,0:T(8,128)S(1)} %get-tuple-element.86), channel_id=1, source_target_pairs={{0,8},{8,16},{16,24},{1,9},{9,17},{17,25},{2,10},{10,18},{18,26},{... | collective-permute-start | bytes 49160 | tf_op jit(solution)/shard_map/ppermute | solution.py:22
  50.6 53.3 %collective-permute-start.18 = (f32[18,1]{1,0:T(8,128)S(1)}, f32[18,1]{1,0:T(8,128)S(1)}, u32[]{:S(2)}, u32[]{:S(2)}) collective-permute-start(f32[18,1]{1,0:T(8,128)S(1)} %get-tuple-element.113), channel_id=1, source_target_pairs={{4,0},{5,1},{6,2},{7,3},{12,8},{13,9},{14,10},{15,11},{20,16},{21,... | collective-permute-start | bytes 224 | tf_op jit(solution)/shard_map/ppermute | solution.py:24
  61.0 13.4 %collective-permute-start.4 = (f32[18,34,1]{2,1,0:T(8,128)S(1)}, f32[18,34,1]{2,1,0:T(8,128)S(1)}, u32[]{:S(2)}, u32[]{:S(2)}) collective-permute-start(f32[18,34,1]{2,1,0:T(8,128)S(1)} %get-tuple-element.57), channel_id=1, source_target_pairs={{1,0},{2,1},{3,2},{5,4},{6,5},{7,6},{9,8},{10,9},{11,10},{13,12},{... | collective-permute-start | bytes 7352 | tf_op jit(solution)/shard_map/ppermute | solution.py:24
  62.3 13.6 %collective-permute-start.5 = (f32[18,34,1]{2,1,0:T(8,128)S(1)}, f32[18,34,1]{2,1,0:T(8,128)S(1)}, u32[]{:S(2)}, u32[]{:S(2)}) collective-permute-start(f32[18,34,1]{2,1,0:T(8,128)S(1)} %get-tuple-element.58), channel_id=1, source_target_pairs={{0,1},{1,2},{2,3},{4,5},{5,6},{6,7},{8,9},{9,10},{10,11},{12,13},{... | collective-permute-start | bytes 7352 | tf_op jit(solution)/shard_map/ppermute | solution.py:22
  67.2 13.5 %collective-permute-start.76 = (f32[18,34,1]{2,1,0:T(8,128)S(1)}, f32[18,34,1]{2,1,0:T(8,128)S(1)}, u32[]{:S(2)}, u32[]{:S(2)}) collective-permute-start(f32[18,34,1]{2,1,0:T(8,128)S(1)} %get-tuple-element.59), channel_id=1, source_target_pairs={{1,0},{2,1},{3,2},{5,4},{6,5},{7,6},{9,8},{10,9},{11,10},{13,12},{... | collective-permute-start | bytes 7352 | tf_op jit(solution)/shard_map/ppermute | solution.py:24
  68.6 13.4 %collective-permute-start.77 = (f32[18,34,1]{2,1,0:T(8,128)S(1)}, f32[18,34,1]{2,1,0:T(8,128)S(1)}, u32[]{:S(2)}, u32[]{:S(2)}) collective-permute-start(f32[18,34,1]{2,1,0:T(8,128)S(1)} %get-tuple-element.60), channel_id=1, source_target_pairs={{0,1},{1,2},{2,3},{4,5},{5,6},{6,7},{8,9},{9,10},{10,11},{12,13},{... | collective-permute-start | bytes 7352 | tf_op jit(solution)/shard_map/ppermute | solution.py:22
  74.4 29.5 %collective-permute-start.19 = (f32[18,1]{1,0:T(8,128)S(1)}, f32[18,1]{1,0:T(8,128)S(1)}, u32[]{:S(2)}, u32[]{:S(2)}) collective-permute-start(f32[18,1]{1,0:T(8,128)S(1)} %get-tuple-element.114), channel_id=1, source_target_pairs={{0,4},{1,5},{2,6},{3,7},{8,12},{9,13},{10,14},{11,15},{16,20},{17,... | collective-permute-start | bytes 224 | tf_op jit(solution)/shard_map/ppermute | solution.py:22
  75.9 36.9 %collective-permute-start.62 = (f32[18,1]{1,0:T(8,128)S(1)}, f32[18,1]{1,0:T(8,128)S(1)}, u32[]{:S(2)}, u32[]{:S(2)}) collective-permute-start(f32[18,1]{1,0:T(8,128)S(1)} %get-tuple-element.105), channel_id=1, source_target_pairs={{4,0},{5,1},{6,2},{7,3},{12,8},{13,9},{14,10},{15,11},{20,16},{21,... | collective-permute-start | bytes 224 | tf_op jit(solution)/shard_map/ppermute | solution.py:24
  80.7 37.6 %collective-permute-start.63 = (f32[18,1]{1,0:T(8,128)S(1)}, f32[18,1]{1,0:T(8,128)S(1)}, u32[]{:S(2)}, u32[]{:S(2)}) collective-permute-start(f32[18,1]{1,0:T(8,128)S(1)} %get-tuple-element.106), channel_id=1, source_target_pairs={{0,4},{1,5},{2,6},{3,7},{8,12},{9,13},{10,14},{11,15},{16,20},{17,... | collective-permute-start | bytes 224 | tf_op jit(solution)/shard_map/ppermute | solution.py:22
  104.0 15.7 %collective-permute-start.26 = (f32[1,32]{1,0:T(1,128)S(1)}, f32[1,32]{1,0:T(1,128)S(1)}, u32[]{:S(2)}, u32[]{:S(2)}) collective-permute-start(f32[1,32]{1,0:T(1,128)S(1)} %get-tuple-element.144), channel_id=1, source_target_pairs={{8,0},{16,8},{24,16},{9,1},{17,9},{25,17},{10,2},{18,10},{26,18},{... | collective-permute-start | bytes 392 | tf_op jit(solution)/shard_map/ppermute | solution.py:24
  105.3 15.7 %collective-permute-start.27 = (f32[1,32]{1,0:T(1,128)S(1)}, f32[1,32]{1,0:T(1,128)S(1)}, u32[]{:S(2)}, u32[]{:S(2)}) collective-permute-start(f32[1,32]{1,0:T(1,128)S(1)} %get-tuple-element.143), channel_id=1, source_target_pairs={{0,8},{8,16},{16,24},{1,9},{9,17},{17,25},{2,10},{10,18},{18,26},{... | collective-permute-start | bytes 392 | tf_op jit(solution)/shard_map/ppermute | solution.py:22
  111.4 77.5 %collective-permute-start.86 = (f32[1,32,128]{2,1,0:T(8,128)S(1)}, f32[1,32,128]{2,1,0:T(8,128)S(1)}, u32[]{:S(2)}, u32[]{:S(2)}) collective-permute-start(f32[1,32,128]{2,1,0:T(8,128)S(1)} %get-tuple-element.74), channel_id=1, source_target_pairs={{8,0},{16,8},{24,16},{9,1},{17,9},{25,17},{10,2},{18,10},{26,18},{... | collective-permute-start | bytes 49160 | tf_op jit(solution)/shard_map/ppermute | solution.py:24
  112.8 77.4 %collective-permute-start.87 = (f32[1,32,128]{2,1,0:T(8,128)S(1)}, f32[1,32,128]{2,1,0:T(8,128)S(1)}, u32[]{:S(2)}, u32[]{:S(2)}) collective-permute-start(f32[1,32,128]{2,1,0:T(8,128)S(1)} %get-tuple-element.73), channel_id=1, source_target_pairs={{0,8},{8,16},{16,24},{1,9},{9,17},{17,25},{2,10},{10,18},{18,26},{... | collective-permute-start | bytes 49160 | tf_op jit(solution)/shard_map/ppermute | solution.py:22
  118.3 63.3 %collective-permute-start.6 = (f32[1,32,128]{2,1,0:T(8,128)S(1)}, f32[1,32,128]{2,1,0:T(8,128)S(1)}, u32[]{:S(2)}, u32[]{:S(2)}) collective-permute-start(f32[1,32,128]{2,1,0:T(8,128)S(1)} %get-tuple-element.82), channel_id=1, source_target_pairs={{8,0},{16,8},{24,16},{9,1},{17,9},{25,17},{10,2},{18,10},{26,18},{... | collective-permute-start | bytes 49160 | tf_op jit(solution)/shard_map/ppermute | solution.py:24
  180.2 89.7 %collective-permute-start.70 = (f32[18,1]{1,0:T(8,128)S(1)}, f32[18,1]{1,0:T(8,128)S(1)}, u32[]{:S(2)}, u32[]{:S(2)}) collective-permute-start(f32[18,1]{1,0:T(8,128)S(1)} %get-tuple-element.97), channel_id=1, source_target_pairs={{4,0},{5,1},{6,2},{7,3},{12,8},{13,9},{14,10},{15,11},{20,16},{21,... | collective-permute-start | bytes 224 | tf_op jit(solution)/shard_map/ppermute | solution.py:24
  186.0 83.9 %collective-permute-start.71 = (f32[18,1]{1,0:T(8,128)S(1)}, f32[18,1]{1,0:T(8,128)S(1)}, u32[]{:S(2)}, u32[]{:S(2)}) collective-permute-start(f32[18,1]{1,0:T(8,128)S(1)} %get-tuple-element.98), channel_id=1, source_target_pairs={{0,4},{1,5},{2,6},{3,7},{8,12},{9,13},{10,14},{11,15},{16,20},{17,... | collective-permute-start | bytes 224 | tf_op jit(solution)/shard_map/ppermute | solution.py:22
  187.3 75.1 %collective-permute-start.46 = (f32[18,1]{1,0:T(8,128)S(1)}, f32[18,1]{1,0:T(8,128)S(1)}, u32[]{:S(2)}, u32[]{:S(2)}) collective-permute-start(f32[18,1]{1,0:T(8,128)S(1)} %get-tuple-element.101), channel_id=1, source_target_pairs={{4,0},{5,1},{6,2},{7,3},{12,8},{13,9},{14,10},{15,11},{20,16},{21,... | collective-permute-start | bytes 224 | tf_op jit(solution)/shard_map/ppermute | solution.py:24
  188.9 13.2 %collective-permute-start.10 = (f32[18,34,1]{2,1,0:T(8,128)S(1)}, f32[18,34,1]{2,1,0:T(8,128)S(1)}, u32[]{:S(2)}, u32[]{:S(2)}) collective-permute-start(f32[18,34,1]{2,1,0:T(8,128)S(1)} %get-tuple-element.55), channel_id=1, source_target_pairs={{1,0},{2,1},{3,2},{5,4},{6,5},{7,6},{9,8},{10,9},{11,10},{13,12},{... | collective-permute-start | bytes 7352 | tf_op jit(solution)/shard_map/ppermute | solution.py:24
  190.2 13.4 %collective-permute-start.11 = (f32[18,34,1]{2,1,0:T(8,128)S(1)}, f32[18,34,1]{2,1,0:T(8,128)S(1)}, u32[]{:S(2)}, u32[]{:S(2)}) collective-permute-start(f32[18,34,1]{2,1,0:T(8,128)S(1)} %get-tuple-element.56), channel_id=1, source_target_pairs={{0,1},{1,2},{2,3},{4,5},{5,6},{6,7},{8,9},{9,10},{10,11},{12,13},{... | collective-permute-start | bytes 7352 | tf_op jit(solution)/shard_map/ppermute | solution.py:22
  219.1 11.8 %collective-permute-start.90 = (f32[18,34,1]{2,1,0:T(8,128)S(1)}, f32[18,34,1]{2,1,0:T(8,128)S(1)}, u32[]{:S(2)}, u32[]{:S(2)}) collective-permute-start(f32[18,34,1]{2,1,0:T(8,128)S(1)} %get-tuple-element.49), channel_id=1, source_target_pairs={{1,0},{2,1},{3,2},{5,4},{6,5},{7,6},{9,8},{10,9},{11,10},{13,12},{... | collective-permute-start | bytes 7352 | tf_op jit(solution)/shard_map/ppermute | solution.py:24
  220.4 11.8 %collective-permute-start.91 = (f32[18,34,1]{2,1,0:T(8,128)S(1)}, f32[18,34,1]{2,1,0:T(8,128)S(1)}, u32[]{:S(2)}, u32[]{:S(2)}) collective-permute-start(f32[18,34,1]{2,1,0:T(8,128)S(1)} %get-tuple-element.50), channel_id=1, source_target_pairs={{0,1},{1,2},{2,3},{4,5},{5,6},{6,7},{8,9},{9,10},{10,11},{12,13},{... | collective-permute-start | bytes 7352 | tf_op jit(solution)/shard_map/ppermute | solution.py:22
  230.9 10.8 %collective-permute-start.24 = (f32[18,34,1]{2,1,0:T(8,128)S(1)}, f32[18,34,1]{2,1,0:T(8,128)S(1)}, u32[]{:S(2)}, u32[]{:S(2)}) collective-permute-start(f32[18,34,1]{2,1,0:T(8,128)S(1)} %get-tuple-element.53), channel_id=1, source_target_pairs={{1,0},{2,1},{3,2},{5,4},{6,5},{7,6},{9,8},{10,9},{11,10},{13,12},{... | collective-permute-start | bytes 7352 | tf_op jit(solution)/shard_map/ppermute | solution.py:24
  241.7 20.7 %collective-permute-start.47 = (f32[18,1]{1,0:T(8,128)S(1)}, f32[18,1]{1,0:T(8,128)S(1)}, u32[]{:S(2)}, u32[]{:S(2)}) collective-permute-start(f32[18,1]{1,0:T(8,128)S(1)} %get-tuple-element.102), channel_id=1, source_target_pairs={{0,4},{1,5},{2,6},{3,7},{8,12},{9,13},{10,14},{11,15},{16,20},{17,... | collective-permute-start | bytes 224 | tf_op jit(solution)/shard_map/ppermute | solution.py:22
  263.2 15.9 %collective-permute-start.48 = (f32[1,32]{1,0:T(1,128)S(1)}, f32[1,32]{1,0:T(1,128)S(1)}, u32[]{:S(2)}, u32[]{:S(2)}) collective-permute-start(f32[1,32]{1,0:T(1,128)S(1)} %get-tuple-element.122), channel_id=1, source_target_pairs={{8,0},{16,8},{24,16},{9,1},{17,9},{25,17},{10,2},{18,10},{26,18},{... | collective-permute-start | bytes 392 | tf_op jit(solution)/shard_map/ppermute | solution.py:24
  264.5 14.7 %collective-permute-start.49 = (f32[1,32]{1,0:T(1,128)S(1)}, f32[1,32]{1,0:T(1,128)S(1)}, u32[]{:S(2)}, u32[]{:S(2)}) collective-permute-start(f32[1,32]{1,0:T(1,128)S(1)} %get-tuple-element.121), channel_id=1, source_target_pairs={{0,8},{8,16},{16,24},{1,9},{9,17},{17,25},{2,10},{10,18},{18,26},{... | collective-permute-start | bytes 392 | tf_op jit(solution)/shard_map/ppermute | solution.py:22
  277.8 47.2 %collective-permute-start.34 = (f32[1,32,128]{2,1,0:T(8,128)S(1)}, f32[1,32,128]{2,1,0:T(8,128)S(1)}, u32[]{:S(2)}, u32[]{:S(2)}) collective-permute-start(f32[1,32,128]{2,1,0:T(8,128)S(1)} %get-tuple-element.76), channel_id=1, source_target_pairs={{8,0},{16,8},{24,16},{9,1},{17,9},{25,17},{10,2},{18,10},{26,18},{... | collective-permute-start | bytes 49160 | tf_op jit(solution)/shard_map/ppermute | solution.py:24
  291.9 19.8 %collective-permute-start.50 = (f32[18,1]{1,0:T(8,128)S(1)}, f32[18,1]{1,0:T(8,128)S(1)}, u32[]{:S(2)}, u32[]{:S(2)}) collective-permute-start(f32[18,1]{1,0:T(8,128)S(1)} %get-tuple-element.89), channel_id=1, source_target_pairs={{4,0},{5,1},{6,2},{7,3},{12,8},{13,9},{14,10},{15,11},{20,16},{21,... | collective-permute-start | bytes 224 | tf_op jit(solution)/shard_map/ppermute | solution.py:24
  313.3 11.8 %collective-permute-start.52 = (f32[1,32]{1,0:T(1,128)S(1)}, f32[1,32]{1,0:T(1,128)S(1)}, u32[]{:S(2)}, u32[]{:S(2)}) collective-permute-start(f32[1,32]{1,0:T(1,128)S(1)} %get-tuple-element.120), channel_id=1, source_target_pairs={{8,0},{16,8},{24,16},{9,1},{17,9},{25,17},{10,2},{18,10},{26,18},{... | collective-permute-start | bytes 392 | tf_op jit(solution)/shard_map/ppermute | solution.py:24
  335.4 11.8 %collective-permute-start.38 = (f32[18,34,1]{2,1,0:T(8,128)S(1)}, f32[18,34,1]{2,1,0:T(8,128)S(1)}, u32[]{:S(2)}, u32[]{:S(2)}) collective-permute-start(f32[18,34,1]{2,1,0:T(8,128)S(1)} %get-tuple-element.51), channel_id=1, source_target_pairs={{1,0},{2,1},{3,2},{5,4},{6,5},{7,6},{9,8},{10,9},{11,10},{13,12},{... | collective-permute-start | bytes 7352 | tf_op jit(solution)/shard_map/ppermute | solution.py:24
  336.7 11.7 %collective-permute-start.39 = (f32[18,34,1]{2,1,0:T(8,128)S(1)}, f32[18,34,1]{2,1,0:T(8,128)S(1)}, u32[]{:S(2)}, u32[]{:S(2)}) collective-permute-start(f32[18,34,1]{2,1,0:T(8,128)S(1)} %get-tuple-element.52), channel_id=1, source_target_pairs={{0,1},{1,2},{2,3},{4,5},{5,6},{6,7},{8,9},{9,10},{10,11},{12,13},{... | collective-permute-start | bytes 7352 | tf_op jit(solution)/shard_map/ppermute | solution.py:22
  (78 other events, 553.5 us)
where the time goes:
time: 353 us; the launch traced here: 350 us
  starting transfers between devices  257 us (73%)
  blocking collectives  38.7 us (11%)
  waiting for transfers between devices  36.9 us (10%)
  other arithmetic  10.5 us (3%)
  local copies, waits for them, and re-layouts  3.69 us (1%)
    ppermute x48, starting transfers between devices, padded_2(): lax.ppermute(tail, axis, [(i, (i + 1) % count) for i in range(ends)])  195 us
    ppermute x48, starting transfers between devices, padded_2(): lax.ppermute(head, axis, [((i + 1) % count, i) for i in range(ends)])  62 us
    psum x2, blocking collectives, on_device(): react = DRIVE_GAIN * lax.psum(jnp.sum(costate_now * dipole, axis=2), 'gz')  38.7 us
    ppermute x48, waiting for transfers between devices, padded_2(): lax.ppermute(head, axis, [((i + 1) % count, i) for i in range(ends)])  27.2 us
    ppermute x48, waiting for transfers between devices, padded_2(): lax.ppermute(tail, axis, [(i, (i + 1) % count) for i in range(ends)])  9.67 us
  transfers between devices with their start and end apart: 96, of which 18 were waited for; matrix products, arithmetic and copies ran while one was open for 3% of the time, Pallas kernels for 0%

commit v1 on v0

v1 whole, which is shorter than its diff:
```python
import functools

import jax
import jax.numpy as jnp
from jax import lax
from jax.experimental import pallas as pl
from jax.experimental.pallas import tpu as pltpu
from jax.sharding import PartitionSpec as P

STEPS = 4

DRIVE_GAIN = 0.5
LOAD_GAIN = 0.5
BEND_GAIN = 0.035

F32 = jnp.float32
MESH = pl.DeviceIdType.MESH

LEFT = 8
HALF = 64
PAD = 8

KEYS = ("xm", "xp", "ym", "yp", "mm", "pp", "mp", "pm", "zm", "zp", "far")
OPPOSITE = {
    "xm": "xp", "xp": "xm", "ym": "yp", "yp": "ym", "mm": "pp", "pp": "mm",
    "mp": "pm", "pm": "mp", "zm": "zp", "zp": "zm", "far": "far",
}
OFFSET = {
    "xm": (-1, 0, 0), "xp": (1, 0, 0), "ym": (0, -1, 0), "yp": (0, 1, 0),
    "mm": (-1, -1, 0), "pp": (1, 1, 0), "mp": (-1, 1, 0), "pm": (1, -1, 0),
    "zm": (0, 0, -1), "zp": (0, 0, 1),
}


def kernel(counts, *refs):
    (
        a_pprev, a_pnow, a_bprev, a_bnow, a_qprev, a_qnow, a_aprev, a_anow,
        a_speed, a_stiff, a_mask, a_height, a_cells, a_force,
        o_first, o_second, o_afirst, o_asecond, o_grad,
        pold, press, qold, q, speed, field, todo, todo_f, dip,
        bprev, bnow, aprev, anow, stiff, maski, heighti, cells, force,
        packs, uext, sext, wext, curve, out_t, first, af, asec, grad,
        xs, xr, ys, yr, dr, zs, zr, fr,
        in_sem, out_sem, send_sem, recv_sem,
    ) = refs
    nx, ny, nz = speed.shape
    top = PAD + ny
    count_x, count_y, count_z = counts
    rows_y = ny * count_y
    low, high = count_z // 2 - 1, count_z // 2
    gx, gy, gz = (lax.axis_index(a) for a in ("gx", "gy", "gz"))
    me = (gx, gy, gz)

    loads = []
    own = pl.ds(PAD, ny)
    for source, target in (
        (a_qnow, q.at[0]), (a_speed, speed), (a_anow, anow), (a_bnow, bnow), (a_mask, maski),
        (a_stiff, stiff), (a_height, heighti), (a_pnow, press.at[0, :, own, :]),
        (a_aprev, aprev), (a_bprev, bprev), (a_cells, cells), (a_force, force),
        (a_qprev, qold), (a_pprev, pold),
    ):
        copy = pltpu.make_async_copy(source, target, in_sem.at[len(loads)])
        copy.start()
        loads.append(copy)

    def partner(key):
        if key == "far":
            half = count_z // 2
            return (gx, gy, jnp.where(gz < half, gz + half, gz - half))
        return tuple(m + o for m, o in zip(me, OFFSET[key]))

    def exists(key):
        if key == "far":
            return gz >= 0
        good = None
        for m, o, n in zip(me, OFFSET[key], counts):
            if o:
                here = m >= 1 if o < 0 else m <= n - 2
                good = here if good is None else jnp.logical_and(good, here)
        return good

    is_mid = jnp.logical_or(gz == low, gz == high)

    for buffer in (xr, yr, dr, zr, fr, packs):
        buffer[...] = jnp.zeros_like(buffer)
    for buffer in (field, press):
        for row in (0, top):
            if len(buffer.shape) == 3:
                buffer[:, row : row + 8, :] = jnp.zeros((nx, 8, nz), F32)
            else:
                buffer[:, :, row : row + 8, :] = jnp.zeros((buffer.shape[0], nx, 8, nz), F32)

    barrier = pltpu.get_barrier_semaphore()
    for key in KEYS:
        @pl.when(exists(key))
        def _(key=key):
            pl.semaphore_signal(barrier, inc=1, device_id=partner(key), device_id_type=MESH)
    peers = 0
    for key in KEYS:
        peers = peers + exists(key).astype(jnp.int32)
    pl.semaphore_wait(barrier, peers)

    def message(step, key, to):
        index = KEYS.index(OPPOSITE[key])
        side = {"m": 0, "p": 1}
        if key[0] == "x":
            size = (4 * ny, 3 * ny, 2 * ny, 2 * ny)[step]
            source = xs.at[step, side[key[1]], pl.ds(0, size), :]
            target = xr.at[step, 1 - side[key[1]], pl.ds(0, size), :]
        elif key[0] == "y":
            begin = 0 if step < 2 else nx
            size = 2 * nx + 8 - begin + (8 if step == 0 else 0)
            source = ys.at[step, side[key[1]], pl.ds(begin, size), :]
            target = yr.at[step, 1 - side[key[1]], pl.ds(begin, size), :]
        elif key[0] == "z":
            source = zs.at[step, side[key[1]]]
            target = zr.at[step, 1 - side[key[1]]]
        elif key == "far":
            source = zs.at[step, 0, pl.ds(ny, ny), :]
            target = fr.at[step]
        else:
            size = 16 if step == 0 else 8
            source = ys.at[step, side[key[1]], pl.ds(2 * nx, size), :]
            target = dr.at[step, index - 4, pl.ds(0, size), :]
        return pltpu.make_async_remote_copy(
            src_ref=source, dst_ref=target,
            send_sem=send_sem.at[step, KEYS.index(key)], recv_sem=recv_sem.at[step, index],
            device_id=to, device_id_type=MESH,
        )

    def send(step):
        for key in KEYS:
            @pl.when(is_mid if key == "far" else exists(key))
            def _(key=key):
                message(step, key, partner(key)).start()

    def arrive(step, keys):
        for key in keys:
            @pl.when(jnp.logical_not(is_mid) if key == "far" else exists(key))
            def _(key=key):
                message(step, OPPOSITE[key], partner(key)).wait_recv()

    def sent(step):
        for key in KEYS:
            @pl.when(is_mid if key == "far" else exists(key))
            def _(key=key):
                message(step, key, partner(key)).wait_send()

    lane = lax.broadcasted_iota(jnp.int32, (ny, nz), 1)
    first_z, last_z = lane == 0, lane == nz - 1
    zero = jnp.zeros((ny, nz), F32)

    def column(values, at):
        return lax.slice_in_dim(values, at, at + 1, axis=1)

    for copy in loads[2:7] + loads[8:10]:
        copy.wait()
    a, b = LEFT, LEFT + HALF
    mid = LEFT + HALF // 2
    packs[0, a : a + nx, 0:ny] = anow[...]
    packs[0, b : b + nx, 0:ny] = bnow[...]
    packs[1, a : a + nx, 0:ny] = aprev[...]
    packs[1, b : b + nx, 0:ny] = -bprev[...]
    packs[2, a : a + nx, 0:ny] = stiff[...]
    packs[2, b : b + nx, 0:ny] = stiff[...]
    packs[3, a : a + nx, 0:ny] = maski[...].astype(F32)
    packs[3, b : b + nx, 0:ny] = maski[...].astype(F32)
    packs[3, mid : mid + nx, 0:ny] = heighti[...].astype(F32)
    turned = [jnp.transpose(packs[i])[0:ny, :] for i in range(4)]
    backward = lane < HALF
    level = turned[3]
    in_half = jnp.bitwise_and(lane, HALF - 1)
    inside = jnp.logical_and(in_half >= LEFT, in_half < LEFT + nx)
    mask = jnp.where(inside, level, 0.0)
    u = mask * turned[0]
    v = jnp.where(backward, turned[1], mask * turned[1])
    rigid = turned[2]

    depth = (lane + gz * nz).astype(F32)
    for x in range(nx):
        h = column(level, mid + x)
        dip[x] = jnp.where(depth == h + 1.0, 1.0, 0.0) - jnp.where(depth == h - 1.0, 1.0, 0.0)

    def stage_plate(step, u):
        for side in range(2):
            xs[step, side, ny : 2 * ny, :] = u
        ys[step, 0, 2 * nx : 2 * nx + 8, :] = u[0:8]
        ys[step, 1, 2 * nx : 2 * nx + 8, :] = u[ny - 8 : ny]

    def gather_plate(step, target, values, x_row, y_row, d_row):
        def merge(left, centre, right):
            index = lane[0 : centre.shape[0]]
            place = jnp.bitwise_and(index, HALF - 1)
            return jnp.where(
                place < LEFT,
                pltpu.roll(left, nz - nx, 1),
                jnp.where(place < LEFT + nx, centre, pltpu.roll(right, nx, 1)),
            )

        target[PAD : PAD + ny, :] = merge(
            xr[step, 0, x_row : x_row + ny, :], values, xr[step, 1, x_row : x_row + ny, :]
        )
        rows = slice(d_row, d_row + 8)
        slot = {key: KEYS.index(key) - 4 for key in ("mm", "pp", "mp", "pm")}
        target[0:PAD, :] = merge(
            dr[step, slot["mm"], rows, :], yr[step, 0, y_row : y_row + 8, :],
            dr[step, slot["pm"], rows, :],
        )
        target[top : top + 8, :] = merge(
            dr[step, slot["mp"], rows, :], yr[step, 1, y_row : y_row + 8, :],
            dr[step, slot["pp"], rows, :],
        )

    def take_air(step, x, value, packed, forward):
        react, near, far = packed
        where = (b if forward else a) + x
        gain = -LOAD_GAIN if forward else DRIVE_GAIN
        here = lane == where
        total = jnp.sum(value * dip[x], axis=1, keepdims=True) * gain
        react = jnp.where(here, total, react)
        if forward and step >= 2:
            return (react, near, far)
        if forward:
            sending = value
            x_rows, y_rows = slice(2 * ny, 3 * ny), 0
        else:
            sending = speed[x] * value
            field[x, PAD : PAD + ny, :] = sending
            x_rows, y_rows = slice(0, ny), nx
        if x == 0:
            xs[step, 0, x_rows, :] = sending
        if x == nx - 1:
            xs[step, 1, x_rows, :] = sending
        ys[step, 0, y_rows + x : y_rows + x + 1, :] = sending[0:1]
        ys[step, 1, y_rows + x : y_rows + x + 1, :] = sending[ny - 1 : ny]
        near = jnp.where(here, column(sending, 0), near)
        far = jnp.where(here, column(sending, nz - 1), far)
        return (react, near, far)

    def stage_z(step, packed):
        react, near, far = packed
        zs[step, 0, 0:ny, :] = near
        zs[step, 1, 0:ny, :] = far
        zs[step, 0, ny : 2 * ny, :] = react
        zs[step, 1, ny : 2 * ny, :] = react

    stage_plate(0, u)
    for side in range(2):
        xs[0, side, 3 * ny : 4 * ny, :] = rigid
    ys[0, 0, 2 * nx + 8 : 2 * nx + 16, :] = rigid[0:8]
    ys[0, 1, 2 * nx + 8 : 2 * nx + 16, :] = rigid[ny - 8 : ny]
    packed = (zero, zero, zero)
    for copy in loads[0:2] + loads[7:8]:
        copy.wait()
    for x in range(nx):
        packed = take_air(0, x, q[0, x], packed, False)
        packed = take_air(0, x, press[0, x, PAD : PAD + ny, :], packed, True)
    stage_z(0, packed)
    send(0)

    for copy in loads[10:12]:
        copy.wait()
    points = cells.shape[1]
    spot = jnp.broadcast_to(cells[...], (nz, points))
    column_x = gx * nx + lax.broadcasted_iota(jnp.int32, (nz, points), 0) - b
    begin = column_x * rows_y
    hit_x = (spot >= begin) & (spot < begin + rows_y)
    hit_x = hit_x & (column_x >= gx * nx) & (column_x < gx * nx + nx)
    spot_y = jnp.broadcast_to(cells[...], (ny, points))
    if rows_y & (rows_y - 1) == 0:
        spot_y = jnp.bitwise_and(spot_y, rows_y - 1)
    else:
        spot_y = lax.rem(spot_y, rows_y)
    hit_y = spot_y == gy * ny + lax.broadcasted_iota(jnp.int32, (ny, points), 0)
    hit_x = jnp.where(hit_x, 1.0, 0.0).astype(F32)
    forcing = [
        lax.dot_general(
            jnp.where(hit_y, jnp.broadcast_to(force[t : t + 1, :], (ny, points)), 0.0),
            hit_x, (((1,), (1,)), ((), ())),
            precision=lax.Precision.HIGHEST, preferred_element_type=F32,
        )
        for t in range(STEPS - 1)
    ]
    for copy in loads[12:14]:
        copy.wait()

    def inner(ref, x):
        centre = ref[x, PAD : PAD + ny, :]
        total = ref[x, PAD - 1 : PAD - 1 + ny, :] + ref[x, PAD + 1 : PAD + 1 + ny, :]
        if x > 0:
            total = total + ref[x - 1, PAD : PAD + ny, :]
        if x < nx - 1:
            total = total + ref[x + 1, PAD : PAD + ny, :]
        total = total + jnp.where(first_z, 0.0, pltpu.roll(centre, 1, 1))
        total = total + jnp.where(last_z, 0.0, pltpu.roll(centre, nz - 1, 1))
        return total - 6.0 * centre

    for step in range(STEPS):
        pull = LOAD_GAIN * u
        drive = DRIVE_GAIN * (u + v)
        for x in range(nx):
            now = q[step, x]
            old = qold[x] if step == 0 else -q[step - 1, x]
            todo[x] = old + 2.0 * now + inner(field, x) - column(pull, a + x) * dip[x]
            if step < 2:
                now = press[step, x, PAD : PAD + ny, :]
                old = pold[x] if step == 0 else press[step - 1, x, PAD : PAD + ny, :]
                todo_f[x] = (
                    2.0 * now - old + speed[x] * inner(press.at[step], x)
                    + column(drive, b + x) * dip[x]
                )
        if step == STEPS - 1:
            for x in range(nx):
                first[x] = -q[step, x]
            copy_first = pltpu.make_async_copy(first, o_first, out_sem.at[0])
            copy_first.start()
        arrive(step, KEYS)

        gather_plate(step, uext, u, ny, 2 * nx, 0)
        if step == 0:
            gather_plate(step, sext, rigid, 3 * ny, 2 * nx + 8, 8)
        wide = slice(PAD - 4, PAD + ny + 4)
        centre = uext[wide, :]
        bend = (
            uext[PAD - 5 : PAD + ny + 3, :] + uext[PAD - 3 : PAD + ny + 5, :]
            + pltpu.roll(centre, 1, 1) + pltpu.roll(centre, nz - 1, 1) - 4.0 * centre
        )
        curve[step, wide, :] = bend
        wext[wide, :] = sext[wide, :] * bend
        centre = wext[PAD : PAD + ny, :]
        bent = (
            wext[PAD - 1 : PAD - 1 + ny, :] + wext[PAD + 1 : PAD + 1 + ny, :]
            + pltpu.roll(centre, 1, 1) + pltpu.roll(centre, nz - 1, 1) - 4.0 * centre
        )
        mine = packed[0]
        react = jnp.where(is_mid, mine, fr[step]) + jnp.where(
            gz <= low, zr[step, 1, ny : 2 * ny, :], zr[step, 0, ny : 2 * ny, :]
        )
        fresh = 2.0 * u + v - BEND_GAIN * bent + react
        if step < STEPS - 1:
            fresh = fresh + forcing[step]
        v = -u - jnp.where(backward, react, 0.0)
        u = mask * fresh
        if step < STEPS - 1:
            stage_plate(step + 1, u)

        packed = (zero, zero, zero)
        for x in range(nx):
            for row, side in ((0, 0), (ny - 1, 1)):
                todo[x, row : row + 1, :] = (
                    todo[x, row : row + 1, :] + yr[step, side, nx + x : nx + x + 1, :]
                )
                if step < 2:
                    todo_f[x, row : row + 1, :] = (
                        todo_f[x, row : row + 1, :]
                        + speed[x, row : row + 1, :] * yr[step, side, x : x + 1, :]
                    )
        below, above = zr[step, 0, 0:ny, :], zr[step, 1, 0:ny, :]

        def outer(x, base, x_rows):
            layer = jnp.where(first_z, column(below, base + x), 0.0)
            layer = jnp.where(last_z, column(above, base + x), layer)
            if x == 0:
                layer = layer + xr[step, 0, x_rows, :]
            if x == nx - 1:
                layer = layer + xr[step, 1, x_rows, :]
            return layer

        for x in range(nx):
            new = todo[x] + outer(x, a, slice(0, ny))
            q[step + 1, x] = new
            if step < STEPS - 1:
                packed = take_air(step + 1, x, new, packed, False)
            if step < 2:
                new = todo_f[x] + speed[x] * outer(x, b, slice(2 * ny, 3 * ny))
                if step == 0:
                    press[1, x, PAD : PAD + ny, :] = new
                packed = take_air(step + 1, x, new, packed, True)
        if step < STEPS - 1:
            stage_z(step + 1, packed)
            send(step + 1)

    copy_second = pltpu.make_async_copy(q.at[STEPS], o_second, out_sem.at[1])
    copy_second.start()
    slope = zero
    for step in range(STEPS):
        slope = slope + curve[STEPS - 1 - step, PAD : PAD + ny, :] * pltpu.roll(
            curve[step, PAD : PAD + ny, :], nz - HALF, 1
        )
    slope = -BEND_GAIN * slope
    third = nz // 4
    out = jnp.where(lane < third, v, jnp.where(lane < 2 * third, pltpu.roll(fresh, third, 1), pltpu.roll(slope, 2 * third, 1)))
    out_t[...] = jnp.zeros_like(out_t)
    out_t[0:ny, :] = out
    done = jnp.transpose(out_t[...])
    af[...] = done[LEFT : LEFT + nx, 0:ny]
    asec[...] = done[LEFT + third : LEFT + third + nx, 0:ny]
    grad[...] = done[LEFT + 2 * third : LEFT + 2 * third + nx, 0:ny]
    stores = [copy_first, copy_second]
    for source, target in ((af, o_afirst), (asec, o_asecond), (grad, o_grad)):
        copy = pltpu.make_async_copy(source, target, out_sem.at[len(stores)])
        copy.start()
        stores.append(copy)
    for step in range(STEPS):
        sent(step)
    for copy in stores:
        copy.wait()


def on_device(counts, press_prev, press_now, board_prev, board_now, costate_prev, costate_now,
              adjoint_prev, adjoint_now, speed, stiffness, plate_mask, height, source_cells,
              source_force):
    nx, ny, nz = speed.shape
    assert counts[2] == 4 and nz == 128 and nx == 16 and ny % 8 == 0
    points = source_cells.shape[0]
    air = jax.ShapeDtypeStruct((nx, ny, nz), F32)
    plate = jax.ShapeDtypeStruct((nx, ny), F32)
    tall = ny + 2 * PAD
    vmem = pltpu.VMEM
    sheet = vmem((nx, ny), F32)
    block = vmem((nx, ny, nz), F32)
    scratch = [
        block, vmem((2, nx, tall, nz), F32), block, vmem((STEPS + 1, nx, ny, nz), F32), block,
        vmem((nx, tall, nz), F32), block, block, block,
        sheet, sheet, sheet, sheet, sheet, vmem((nx, ny), jnp.int32), vmem((nx, ny), jnp.int32),
        vmem((1, points), jnp.int32), vmem(source_force.shape, F32),
        vmem((4, nz, nz), F32), vmem((tall, nz), F32), vmem((tall, nz), F32),
        vmem((tall, nz), F32), vmem((STEPS, tall, nz), F32), vmem((nz, nz), F32),
        block, sheet, sheet, sheet,
        vmem((STEPS, 2, 4 * ny, nz), F32), vmem((STEPS, 2, 4 * ny, nz), F32),
        vmem((STEPS, 2, 2 * nx + 16, nz), F32), vmem((STEPS, 2, 2 * nx + 16, nz), F32),
        vmem((STEPS, 4, 16, nz), F32),
        vmem((STEPS, 2, 2 * ny, nz), F32), vmem((STEPS, 2, 2 * ny, nz), F32),
        vmem((STEPS, ny, nz), F32),
        pltpu.SemaphoreType.DMA((14,)), pltpu.SemaphoreType.DMA((5,)),
        pltpu.SemaphoreType.DMA((STEPS, len(KEYS))), pltpu.SemaphoreType.DMA((STEPS, len(KEYS))),
    ]
    anywhere = pl.BlockSpec(memory_space=pl.ANY)
    return pl.pallas_call(
        functools.partial(kernel, counts),
        out_shape=(air, air, plate, plate, plate),
        in_specs=[anywhere] * 14,
        out_specs=(anywhere,) * 5,
        scratch_shapes=scratch,
        compiler_params=pltpu.CompilerParams(
            collective_id=0, has_side_effects=True, vmem_limit_bytes=40 * 1024 * 1024
        ),
        cost_estimate=pl.CostEstimate(
            flops=40 * 6 * nx * ny * nz, bytes_accessed=28 * nx * ny * nz, transcendentals=0
        ),
    )(
        press_prev, press_now, board_prev, board_now, costate_prev, costate_now, adjoint_prev,
        adjoint_now, speed, stiffness, plate_mask, height, source_cells.reshape(1, points),
        source_force,
    )


def solution(mesh):
    air, plate = P("gx", "gy", "gz"), P("gx", "gy")
    counts = tuple(mesh.shape[a] for a in ("gx", "gy", "gz"))
    return jax.shard_map(
        functools.partial(on_device, counts),
        mesh=mesh,
        in_specs=(air, air, plate, plate, air, air, plate, plate, air, plate, plate, plate, P(), P()),
        out_specs=(air, air, plate, plate, plate),
        check_vma=False,
    )
```

time: 353 us -> 47.7 us (0.14)
  starting transfers between devices: 257 us -> 0 us
  blocking collectives: 38.7 us -> 0 us
  waiting for transfers between devices: 36.9 us -> 0 us
  Pallas kernels: 0 us -> 32.2 us
  local copies, waits for them, and re-layouts: 3.69 us -> 14.2 us
  other arithmetic: 10.5 us -> 0 us
    ppermute x96 -> x0, starting transfers between devices: 257 us -> none  [the longest x48 195 us: padded_2(): lax.ppermute(tail, axis, [(i, (i + 1) % count) for i in range(ends)])]
    psum x2 -> x0, blocking collectives: 38.7 us -> none  [on_device(): react = DRIVE_GAIN * lax.psum(jnp.sum(costate_now * dipole, axis=2), 'gz')]
    ppermute x96 -> x0, waiting for transfers between devices: 36.9 us -> none  [the longest x48 27.2 us: padded_2(): lax.ppermute(head, axis, [((i + 1) % count, i) for i in range(ends)])]
    pallas_call x0 -> x1, Pallas kernels: none -> 32.2 us  [on_device(): pl.pallas_call(functools.partial(kernel, counts), out_shape=(air, air, pl...]
    unnamed x30 -> x33, local copies, waits for them, and re-layouts: 1.42 us -> 14.2 us
  transfers between devices with their start and end apart: 96 -> 0, of which waited for: 18 -> 0; matrix products, arithmetic and copies ran while one was open for 3% -> 0% of each run, Pallas kernels for 0% -> 0%
where the time goes in v1:
time: 47.7 us; the launch traced here: 47.1 us
  Pallas kernels  32.2 us (68%)
  local copies, waits for them, and re-layouts  14.2 us (30%)
  between operations  0.67 us (1%)
    pallas_call x1, Pallas kernels, on_device(): pl.pallas_call(functools.partial(kernel, counts), out_shape=(air, air, pl...  32.2 us
    unnamed x33, local copies, waits for them, and re-layouts  14.2 us

profile of v1, /device:TPU:0, one launch (start us, length us, event | category | flops | bytes accessed | tf_op | source)
XLA Modules:
  0.0 47.1 jit_solution(10246618630609350806)
XLA Ops:
  0.6 0.0 copy-start.13
  0.6 0.6 %copy-done.13 = s32[88]{0:T(128)S(1)} copy-done((s32[88]{0:T(128)S(1)}, s32[88]{0:T(128)}, u32[]{:S(2)}) %copy-start.13) | copy-done | bytes 376
  1.3 0.0 copy-start
  1.3 0.9 %copy-done = f32[16,32,128]{2,1,0:T(8,128)S(1)} copy-done((f32[16,32,128]{2,1,0:T(8,128)S(1)}, f32[16,32,128]{2,1,0:T(8,128)}, u32[]{:S(2)}) %copy-start) | copy-done | bytes 262168
  2.2 0.0 copy-start.1
  2.2 0.9 %copy-done.1 = f32[16,32,128]{2,1,0:T(8,128)S(1)} copy-done((f32[16,32,128]{2,1,0:T(8,128)S(1)}, f32[16,32,128]{2,1,0:T(8,128)}, u32[]{:S(2)}) %copy-start.1) | copy-done | bytes 262168
  3.2 0.0 copy-start.2
  3.2 0.9 %copy-done.2 = f32[16,32,128]{2,1,0:T(8,128)S(1)} copy-done((f32[16,32,128]{2,1,0:T(8,128)S(1)}, f32[16,32,128]{2,1,0:T(8,128)}, u32[]{:S(2)}) %copy-start.2) | copy-done | bytes 262168
  4.1 0.0 copy-start.3
  4.1 0.9 %copy-done.3 = f32[16,32,128]{2,1,0:T(8,128)S(1)} copy-done((f32[16,32,128]{2,1,0:T(8,128)S(1)}, f32[16,32,128]{2,1,0:T(8,128)}, u32[]{:S(2)}) %copy-start.3) | copy-done | bytes 262168
  5.1 0.0 copy-start.4
  5.1 0.9 %copy-done.4 = f32[16,32,128]{2,1,0:T(8,128)S(1)} copy-done((f32[16,32,128]{2,1,0:T(8,128)S(1)}, f32[16,32,128]{2,1,0:T(8,128)}, u32[]{:S(2)}) %copy-start.4) | copy-done | bytes 262168
  6.0 0.7 %copy-done.5 = f32[16,32]{1,0:T(8,128)S(1)} copy-done((f32[16,32]{1,0:T(8,128)S(1)}, f32[16,32]{1,0:T(8,128)}, u32[]{:S(2)}) %copy-start.5) | copy-done | bytes 2072
  6.7 0.0 copy-start.6
  6.7 0.7 %copy-done.6 = f32[16,32]{1,0:T(8,128)S(1)} copy-done((f32[16,32]{1,0:T(8,128)S(1)}, f32[16,32]{1,0:T(8,128)}, u32[]{:S(2)}) %copy-start.6) | copy-done | bytes 2072
  7.4 0.0 copy-start.7
  7.4 0.7 %copy-done.7 = f32[16,32]{1,0:T(8,128)S(1)} copy-done((f32[16,32]{1,0:T(8,128)S(1)}, f32[16,32]{1,0:T(8,128)}, u32[]{:S(2)}) %copy-start.7) | copy-done | bytes 2072
  8.1 0.0 copy-start.8
  8.1 0.7 %copy-done.8 = f32[16,32]{1,0:T(8,128)S(1)} copy-done((f32[16,32]{1,0:T(8,128)S(1)}, f32[16,32]{1,0:T(8,128)}, u32[]{:S(2)}) %copy-start.8) | copy-done | bytes 2072
  8.8 0.0 copy-start.9
  8.8 0.7 %copy-done.9 = f32[16,32]{1,0:T(8,128)S(1)} copy-done((f32[16,32]{1,0:T(8,128)S(1)}, f32[16,32]{1,0:T(8,128)}, u32[]{:S(2)}) %copy-start.9) | copy-done | bytes 2072
  9.5 0.0 copy-start.10
  9.5 0.7 %copy-done.10 = s32[16,32]{1,0:T(8,128)S(1)} copy-done((s32[16,32]{1,0:T(8,128)S(1)}, s32[16,32]{1,0:T(8,128)}, u32[]{:S(2)}) %copy-start.10) | copy-done | bytes 2072
  10.2 0.0 copy-start.11
  10.2 0.7 %copy-done.11 = s32[16,32]{1,0:T(8,128)S(1)} copy-done((s32[16,32]{1,0:T(8,128)S(1)}, s32[16,32]{1,0:T(8,128)}, u32[]{:S(2)}) %copy-start.11) | copy-done | bytes 2072
  10.9 0.7 %copy-done.12 = f32[4,88]{1,0:T(4,128)S(1)} copy-done((f32[4,88]{1,0:T(4,128)S(1)}, f32[4,88]{1,0:T(4,128)}, u32[]{:S(2)}) %copy-start.12) | copy-done | bytes 1432
  11.6 32.2 %shard_map.173 = (f32[16,32,128]{2,1,0:T(8,128)S(1)}, f32[16,32,128]{2,1,0:T(8,128)S(1)}, f32[16,32]{1,0:T(8,128)S(1)}, f32[16,32]{1,0:T(8,128)S(1)}, f32[16,32]{1,0:T(8,128)S(1)}) custom-call(f32[16,32,128]{2,1,0:T(8,128)S(1)} %copy-done, f32[16,32,128]{2,1,0:T(8,128)S(1)} %copy-done.1, f32[16,32]{1,0:T(8,128)S(1)} %copy-done.5, f32[16,32]{1,0:T(8,128)S(1)} %copy-done.6, ...), custom_call_target="tpu_custom_call" | custom-call | flops 15728640 | bytes 1835008 | tf_op jit(solution)/shard_map/pallas_call | solution.py:439
  43.9 0.7 %copy.24 = f32[16,32,128]{2,1,0:T(8,128)} copy(f32[16,32,128]{2,1,0:T(8,128)S(1)} %get-tuple-element.10) | data formatting | bytes 524288
  44.6 0.7 %copy.25 = f32[16,32,128]{2,1,0:T(8,128)} copy(f32[16,32,128]{2,1,0:T(8,128)S(1)} %get-tuple-element.11) | data formatting | bytes 524288
  45.3 0.6 %copy.26 = f32[16,32]{1,0:T(8,128)} copy(f32[16,32]{1,0:T(8,128)S(1)} %get-tuple-element.12) | data formatting | bytes 4096
  45.9 0.6 %copy.27 = f32[16,32]{1,0:T(8,128)} copy(f32[16,32]{1,0:T(8,128)S(1)} %get-tuple-element.13) | data formatting | bytes 4096
  46.5 0.6 %copy.28 = f32[16,32]{1,0:T(8,128)} copy(f32[16,32]{1,0:T(8,128)S(1)} %get-tuple-element.14) | data formatting | bytes 4096
  (2 shorter events, 0.0 us)
Async XLA Ops:
  0.6 0.7 %copy-start.13 = (s32[88]{0:T(128)S(1)}, s32[88]{0:T(128)}, u32[]{:S(2)}) copy-start(s32[88]{0:T(128)} %param.26) | copy-start | bytes 1060
  1.3 0.9 %copy-start = (f32[16,32,128]{2,1,0:T(8,128)S(1)}, f32[16,32,128]{2,1,0:T(8,128)}, u32[]{:S(2)}) copy-start(f32[16,32,128]{2,1,0:T(8,128)} %refs_0_.1) | copy-start | bytes 786436
  2.2 0.9 %copy-start.1 = (f32[16,32,128]{2,1,0:T(8,128)S(1)}, f32[16,32,128]{2,1,0:T(8,128)}, u32[]{:S(2)}) copy-start(f32[16,32,128]{2,1,0:T(8,128)} %refs_1_.1) | copy-start | bytes 786436
  3.2 0.9 %copy-start.2 = (f32[16,32,128]{2,1,0:T(8,128)S(1)}, f32[16,32,128]{2,1,0:T(8,128)}, u32[]{:S(2)}) copy-start(f32[16,32,128]{2,1,0:T(8,128)} %refs_4_.1) | copy-start | bytes 786436
  4.1 0.9 %copy-start.3 = (f32[16,32,128]{2,1,0:T(8,128)S(1)}, f32[16,32,128]{2,1,0:T(8,128)}, u32[]{:S(2)}) copy-start(f32[16,32,128]{2,1,0:T(8,128)} %refs_5_.1) | copy-start | bytes 786436
  5.1 0.9 %copy-start.4 = (f32[16,32,128]{2,1,0:T(8,128)S(1)}, f32[16,32,128]{2,1,0:T(8,128)}, u32[]{:S(2)}) copy-start(f32[16,32,128]{2,1,0:T(8,128)} %refs_8_.1) | copy-start | bytes 786436
  6.0 0.7 %copy-start.5 = (f32[16,32]{1,0:T(8,128)S(1)}, f32[16,32]{1,0:T(8,128)}, u32[]{:S(2)}) copy-start(f32[16,32]{1,0:T(8,128)} %refs_2_.1) | copy-start | bytes 6148
  6.7 0.7 %copy-start.6 = (f32[16,32]{1,0:T(8,128)S(1)}, f32[16,32]{1,0:T(8,128)}, u32[]{:S(2)}) copy-start(f32[16,32]{1,0:T(8,128)} %refs_3_.1) | copy-start | bytes 6148
  7.4 0.7 %copy-start.7 = (f32[16,32]{1,0:T(8,128)S(1)}, f32[16,32]{1,0:T(8,128)}, u32[]{:S(2)}) copy-start(f32[16,32]{1,0:T(8,128)} %refs_6_.1) | copy-start | bytes 6148
  8.1 0.7 %copy-start.8 = (f32[16,32]{1,0:T(8,128)S(1)}, f32[16,32]{1,0:T(8,128)}, u32[]{:S(2)}) copy-start(f32[16,32]{1,0:T(8,128)} %refs_7_.1) | copy-start | bytes 6148
  8.8 0.7 %copy-start.9 = (f32[16,32]{1,0:T(8,128)S(1)}, f32[16,32]{1,0:T(8,128)}, u32[]{:S(2)}) copy-start(f32[16,32]{1,0:T(8,128)} %refs_9_.1) | copy-start | bytes 6148
  9.5 0.7 %copy-start.10 = (s32[16,32]{1,0:T(8,128)S(1)}, s32[16,32]{1,0:T(8,128)}, u32[]{:S(2)}) copy-start(s32[16,32]{1,0:T(8,128)} %refs_10_.1) | copy-start | bytes 6148
  10.2 0.7 %copy-start.11 = (s32[16,32]{1,0:T(8,128)S(1)}, s32[16,32]{1,0:T(8,128)}, u32[]{:S(2)}) copy-start(s32[16,32]{1,0:T(8,128)} %refs_11_.1) | copy-start | bytes 6148
  10.9 0.7 %copy-start.12 = (f32[4,88]{1,0:T(4,128)S(1)}, f32[4,88]{1,0:T(4,128)}, u32[]{:S(2)}) copy-start(f32[4,88]{1,0:T(4,128)} %refs_13_.1) | copy-start | bytes 4228

commit v2 on v1

--- a/solution.py
+++ b/solution.py
@@ -39,9 +39,9 @@
         o_first, o_second, o_afirst, o_asecond, o_grad,
         pold, press, qold, q, speed, field, todo, todo_f, dip,
         bprev, bnow, aprev, anow, stiff, maski, heighti, cells, force,
-        packs, uext, sext, wext, curve, out_t, first, af, asec, grad,
+        packs, uext, sext, wext, curve, out_t,
         xs, xr, ys, yr, dr, zs, zr, fr,
-        in_sem, out_sem, send_sem, recv_sem,
+        in_sem, send_sem, recv_sem,
     ) = refs
     nx, ny, nz = speed.shape
     top = PAD + ny
@@ -95,18 +95,15 @@
         @pl.when(exists(key))
         def _(key=key):
             pl.semaphore_signal(barrier, inc=1, device_id=partner(key), device_id_type=MESH)
-    peers = 0
-    for key in KEYS:
-        peers = peers + exists(key).astype(jnp.int32)
-    pl.semaphore_wait(barrier, peers)
 
     def message(step, key, to):
         index = KEYS.index(OPPOSITE[key])
         side = {"m": 0, "p": 1}
         if key[0] == "x":
-            size = (4 * ny, 3 * ny, 2 * ny, 2 * ny)[step]
-            source = xs.at[step, side[key[1]], pl.ds(0, size), :]
-            target = xr.at[step, 1 - side[key[1]], pl.ds(0, size), :]
+            begin = 0 if step < 2 else ny
+            size = 2 * ny + 8 - begin + (8 if step == 0 else 0)
+            source = xs.at[step, side[key[1]], pl.ds(begin, size), :]
+            target = xr.at[step, 1 - side[key[1]], pl.ds(begin, size), :]
         elif key[0] == "y":
             begin = 0 if step < 2 else nx
             size = 2 * nx + 8 - begin + (8 if step == 0 else 0)
@@ -116,7 +113,7 @@
             source = zs.at[step, side[key[1]]]
             target = zr.at[step, 1 - side[key[1]]]
         elif key == "far":
-            source = zs.at[step, 0, pl.ds(ny, ny), :]
+            source = zs.at[step, 0]
             target = fr.at[step]
         else:
             size = 16 if step == 0 else 8
@@ -128,8 +125,8 @@
             device_id=to, device_id_type=MESH,
         )
 
-    def send(step):
-        for key in KEYS:
+    def send(step, keys):
+        for key in keys:
             @pl.when(is_mid if key == "far" else exists(key))
             def _(key=key):
                 message(step, key, partner(key)).start()
@@ -181,9 +178,28 @@
         h = column(level, mid + x)
         dip[x] = jnp.where(depth == h + 1.0, 1.0, 0.0) - jnp.where(depth == h - 1.0, 1.0, 0.0)
 
+    def shifted(values, by):
+        by = by % nz
+        return pltpu.roll(values, by, 1) if by else values
+
+    chunk = jnp.bitwise_and(lane[0:8], HALF - 1) // 8
+
+    def edge(values, side):
+        begin = LEFT if side == 0 else LEFT + nx - 8
+        out = zero[0:8]
+        for c in range(ny // 8):
+            out = jnp.where(chunk == c, shifted(values[8 * c : 8 * c + 8], 8 * c - begin), out)
+        return out
+
+    def unfold_edge(values, begin):
+        return jnp.concatenate([shifted(values, begin - 8 * c) for c in range(ny // 8)], axis=0)
+
+    def unfold_z(values):
+        return jnp.concatenate([values, shifted(values, -nx)], axis=0)
+
     def stage_plate(step, u):
         for side in range(2):
-            xs[step, side, ny : 2 * ny, :] = u
+            xs[step, side, 2 * ny : 2 * ny + 8, :] = edge(u, side)
         ys[step, 0, 2 * nx : 2 * nx + 8, :] = u[0:8]
         ys[step, 1, 2 * nx : 2 * nx + 8, :] = u[ny - 8 : ny]
 
@@ -193,22 +209,23 @@
             place = jnp.bitwise_and(index, HALF - 1)
             return jnp.where(
                 place < LEFT,
-                pltpu.roll(left, nz - nx, 1),
-                jnp.where(place < LEFT + nx, centre, pltpu.roll(right, nx, 1)),
+                left,
+                jnp.where(place < LEFT + nx, centre, right),
             )
 
         target[PAD : PAD + ny, :] = merge(
-            xr[step, 0, x_row : x_row + ny, :], values, xr[step, 1, x_row : x_row + ny, :]
+            unfold_edge(xr[step, 0, x_row : x_row + 8, :], LEFT - 8), values,
+            unfold_edge(xr[step, 1, x_row : x_row + 8, :], LEFT + nx),
         )
         rows = slice(d_row, d_row + 8)
         slot = {key: KEYS.index(key) - 4 for key in ("mm", "pp", "mp", "pm")}
         target[0:PAD, :] = merge(
-            dr[step, slot["mm"], rows, :], yr[step, 0, y_row : y_row + 8, :],
-            dr[step, slot["pm"], rows, :],
+            shifted(dr[step, slot["mm"], rows, :], -nx), yr[step, 0, y_row : y_row + 8, :],
+            shifted(dr[step, slot["pm"], rows, :], nx),
         )
         target[top : top + 8, :] = merge(
-            dr[step, slot["mp"], rows, :], yr[step, 1, y_row : y_row + 8, :],
-            dr[step, slot["pp"], rows, :],
+            shifted(dr[step, slot["mp"], rows, :], -nx), yr[step, 1, y_row : y_row + 8, :],
+            shifted(dr[step, slot["pp"], rows, :], nx),
         )
 
     def take_air(step, x, value, packed, forward):
@@ -222,11 +239,11 @@
             return (react, near, far)
         if forward:
             sending = value
-            x_rows, y_rows = slice(2 * ny, 3 * ny), 0
+            x_rows, y_rows = slice(0, ny), 0
         else:
             sending = speed[x] * value
             field[x, PAD : PAD + ny, :] = sending
-            x_rows, y_rows = slice(0, ny), nx
+            x_rows, y_rows = slice(ny, 2 * ny), nx
         if x == 0:
             xs[step, 0, x_rows, :] = sending
         if x == nx - 1:
@@ -239,24 +256,32 @@
 
     def stage_z(step, packed):
         react, near, far = packed
-        zs[step, 0, 0:ny, :] = near
-        zs[step, 1, 0:ny, :] = far
-        zs[step, 0, ny : 2 * ny, :] = react
-        zs[step, 1, ny : 2 * ny, :] = react
+        react = shifted(react, 2 * nx)
+        for side, face in ((0, near), (1, far)):
+            both = face + react
+            zs[step, side] = both[0 : ny // 2] + shifted(both[ny // 2 : ny], nx)
 
     stage_plate(0, u)
     for side in range(2):
-        xs[0, side, 3 * ny : 4 * ny, :] = rigid
+        xs[0, side, 2 * ny + 8 : 2 * ny + 16, :] = edge(rigid, side)
     ys[0, 0, 2 * nx + 8 : 2 * nx + 16, :] = rigid[0:8]
     ys[0, 1, 2 * nx + 8 : 2 * nx + 16, :] = rigid[ny - 8 : ny]
     packed = (zero, zero, zero)
     for copy in loads[0:2] + loads[7:8]:
         copy.wait()
-    for x in range(nx):
+    peers = 0
+    for key in KEYS:
+        peers = peers + exists(key).astype(jnp.int32)
+    pl.semaphore_wait(barrier, peers)
+    send(0, KEYS[4:8])
+    order = (0, nx - 1) + tuple(range(1, nx - 1))
+    for i, x in enumerate(order):
         packed = take_air(0, x, q[0, x], packed, False)
         packed = take_air(0, x, press[0, x, PAD : PAD + ny, :], packed, True)
+        if i == 1:
+            send(0, KEYS[0:2])
     stage_z(0, packed)
-    send(0)
+    send(0, KEYS[8:11] + KEYS[2:4])
 
     for copy in loads[10:12]:
         copy.wait()
@@ -311,14 +336,12 @@
                 )
         if step == STEPS - 1:
             for x in range(nx):
-                first[x] = -q[step, x]
-            copy_first = pltpu.make_async_copy(first, o_first, out_sem.at[0])
-            copy_first.start()
+                o_first[x] = -q[step, x]
         arrive(step, KEYS)
 
-        gather_plate(step, uext, u, ny, 2 * nx, 0)
+        gather_plate(step, uext, u, 2 * ny, 2 * nx, 0)
         if step == 0:
-            gather_plate(step, sext, rigid, 3 * ny, 2 * nx + 8, 8)
+            gather_plate(step, sext, rigid, 2 * ny + 8, 2 * nx + 8, 8)
         wide = slice(PAD - 4, PAD + ny + 4)
         centre = uext[wide, :]
         bend = (
@@ -333,8 +356,9 @@
             + pltpu.roll(centre, 1, 1) + pltpu.roll(centre, nz - 1, 1) - 4.0 * centre
         )
         mine = packed[0]
-        react = jnp.where(is_mid, mine, fr[step]) + jnp.where(
-            gz <= low, zr[step, 1, ny : 2 * ny, :], zr[step, 0, ny : 2 * ny, :]
+        below, above = unfold_z(zr[step, 0]), unfold_z(zr[step, 1])
+        react = jnp.where(is_mid, mine, shifted(unfold_z(fr[step]), -2 * nx)) + shifted(
+            jnp.where(gz <= low, above, below), -2 * nx
         )
         fresh = 2.0 * u + v - BEND_GAIN * bent + react
         if step < STEPS - 1:
@@ -343,6 +367,7 @@
         u = mask * fresh
         if step < STEPS - 1:
             stage_plate(step + 1, u)
+            send(step + 1, KEYS[4:8])
 
         packed = (zero, zero, zero)
         for x in range(nx):
@@ -355,8 +380,6 @@
                         todo_f[x, row : row + 1, :]
                         + speed[x, row : row + 1, :] * yr[step, side, x : x + 1, :]
                     )
-        below, above = zr[step, 0, 0:ny, :], zr[step, 1, 0:ny, :]
-
         def outer(x, base, x_rows):
             layer = jnp.where(first_z, column(below, base + x), 0.0)
             layer = jnp.where(last_z, column(above, base + x), layer)
@@ -366,22 +389,24 @@
                 layer = layer + xr[step, 1, x_rows, :]
             return layer
 
-        for x in range(nx):
-            new = todo[x] + outer(x, a, slice(0, ny))
-            q[step + 1, x] = new
-            if step < STEPS - 1:
+        for i, x in enumerate(order):
+            new = todo[x] + outer(x, a, slice(ny, 2 * ny))
+            if step == STEPS - 1:
+                o_second[x] = new
+            else:
+                q[step + 1, x] = new
                 packed = take_air(step + 1, x, new, packed, False)
             if step < 2:
-                new = todo_f[x] + speed[x] * outer(x, b, slice(2 * ny, 3 * ny))
+                new = todo_f[x] + speed[x] * outer(x, b, slice(0, ny))
                 if step == 0:
                     press[1, x, PAD : PAD + ny, :] = new
                 packed = take_air(step + 1, x, new, packed, True)
+            if i == 1 and step < STEPS - 1:
+                send(step + 1, KEYS[0:2])
         if step < STEPS - 1:
             stage_z(step + 1, packed)
-            send(step + 1)
-
-    copy_second = pltpu.make_async_copy(q.at[STEPS], o_second, out_sem.at[1])
-    copy_second.start()
+            send(step + 1, KEYS[8:11] + KEYS[2:4])
+
     slope = zero
     for step in range(STEPS):
         slope = slope + curve[STEPS - 1 - step, PAD : PAD + ny, :] * pltpu.roll(
@@ -393,25 +418,18 @@
     out_t[...] = jnp.zeros_like(out_t)
     out_t[0:ny, :] = out
     done = jnp.transpose(out_t[...])
-    af[...] = done[LEFT : LEFT + nx, 0:ny]
-    asec[...] = done[LEFT + third : LEFT + third + nx, 0:ny]
-    grad[...] = done[LEFT + 2 * third : LEFT + 2 * third + nx, 0:ny]
-    stores = [copy_first, copy_second]
-    for source, target in ((af, o_afirst), (asec, o_asecond), (grad, o_grad)):
-        copy = pltpu.make_async_copy(source, target, out_sem.at[len(stores)])
-        copy.start()
-        stores.append(copy)
+    o_afirst[...] = done[LEFT : LEFT + nx, 0:ny]
+    o_asecond[...] = done[LEFT + third : LEFT + third + nx, 0:ny]
+    o_grad[...] = done[LEFT + 2 * third : LEFT + 2 * third + nx, 0:ny]
     for step in range(STEPS):
         sent(step)
-    for copy in stores:
-        copy.wait()
 
 
 def on_device(counts, press_prev, press_now, board_prev, board_now, costate_prev, costate_now,
               adjoint_prev, adjoint_now, speed, stiffness, plate_mask, height, source_cells,
               source_force):
     nx, ny, nz = speed.shape
-    assert counts[2] == 4 and nz == 128 and nx == 16 and ny % 8 == 0
+    assert counts[2] == 4 and nz == 128 and nx == 16 and ny % 16 == 0 and ny <= HALF
     points = source_cells.shape[0]
     air = jax.ShapeDtypeStruct((nx, ny, nz), F32)
     plate = jax.ShapeDtypeStruct((nx, ny), F32)
@@ -420,30 +438,30 @@
     sheet = vmem((nx, ny), F32)
     block = vmem((nx, ny, nz), F32)
     scratch = [
-        block, vmem((2, nx, tall, nz), F32), block, vmem((STEPS + 1, nx, ny, nz), F32), block,
+        block, vmem((2, nx, tall, nz), F32), block, vmem((STEPS, nx, ny, nz), F32), block,
         vmem((nx, tall, nz), F32), block, block, block,
         sheet, sheet, sheet, sheet, sheet, vmem((nx, ny), jnp.int32), vmem((nx, ny), jnp.int32),
         vmem((1, points), jnp.int32), vmem(source_force.shape, F32),
         vmem((4, nz, nz), F32), vmem((tall, nz), F32), vmem((tall, nz), F32),
         vmem((tall, nz), F32), vmem((STEPS, tall, nz), F32), vmem((nz, nz), F32),
-        block, sheet, sheet, sheet,
-        vmem((STEPS, 2, 4 * ny, nz), F32), vmem((STEPS, 2, 4 * ny, nz), F32),
+        vmem((STEPS, 2, 2 * ny + 16, nz), F32), vmem((STEPS, 2, 2 * ny + 16, nz), F32),
         vmem((STEPS, 2, 2 * nx + 16, nz), F32), vmem((STEPS, 2, 2 * nx + 16, nz), F32),
         vmem((STEPS, 4, 16, nz), F32),
-        vmem((STEPS, 2, 2 * ny, nz), F32), vmem((STEPS, 2, 2 * ny, nz), F32),
-        vmem((STEPS, ny, nz), F32),
-        pltpu.SemaphoreType.DMA((14,)), pltpu.SemaphoreType.DMA((5,)),
+        vmem((STEPS, 2, ny // 2, nz), F32), vmem((STEPS, 2, ny // 2, nz), F32),
+        vmem((STEPS, ny // 2, nz), F32),
+        pltpu.SemaphoreType.DMA((14,)),
         pltpu.SemaphoreType.DMA((STEPS, len(KEYS))), pltpu.SemaphoreType.DMA((STEPS, len(KEYS))),
     ]
     anywhere = pl.BlockSpec(memory_space=pl.ANY)
-    return pl.pallas_call(
+    resident = pl.BlockSpec(memory_space=pltpu.VMEM)
+    results = pl.pallas_call(
         functools.partial(kernel, counts),
         out_shape=(air, air, plate, plate, plate),
         in_specs=[anywhere] * 14,
-        out_specs=(anywhere,) * 5,
+        out_specs=(resident,) * 5,
         scratch_shapes=scratch,
         compiler_params=pltpu.CompilerParams(
-            collective_id=0, has_side_effects=True, vmem_limit_bytes=40 * 1024 * 1024
+            collective_id=0, has_side_effects=True, vmem_limit_bytes=63 * 1024 * 1024
         ),
         cost_estimate=pl.CostEstimate(
             flops=40 * 6 * nx * ny * nz, bytes_accessed=28 * nx * ny * nz, transcendentals=0
@@ -453,6 +471,26 @@
         adjoint_now, speed, stiffness, plate_mask, height, source_cells.reshape(1, points),
         source_force,
     )
+    return pl.pallas_call(
+        hand_out,
+        out_shape=(air, air, plate, plate, plate),
+        in_specs=[resident] * 5,
+        out_specs=(anywhere,) * 5,
+        scratch_shapes=[pltpu.SemaphoreType.DMA((5,))],
+        compiler_params=pltpu.CompilerParams(vmem_limit_bytes=62 * 1024 * 1024),
+    )(*results)
+
+
+def hand_out(*refs):
+    sources, targets, sem = refs[:5], refs[5:10], refs[10]
+    copies = [
+        pltpu.make_async_copy(source, target, sem.at[i])
+        for i, (source, target) in enumerate(zip(sources, targets))
+    ]
+    for copy in copies:
+        copy.start()
+    for copy in copies:
+        copy.wait()
 
 
 def solution(mesh):

time: 47.7 us -> 29.7 us (0.62)
  local copies, waits for them, and re-layouts: 14.2 us -> 0 us
  Pallas kernels: 32.2 us -> 28.9 us
    unnamed x33 -> x0, local copies, waits for them, and re-layouts: 14.2 us -> none
    pallas_call x1, Pallas kernels: 32.2 us -> 27 us  [on_device(): pl.pallas_call(functools.partial(kernel, counts), out_shape=(air, air, pl...]
    pallas_call x0 -> x1, Pallas kernels: none -> 1.89 us  [on_device(): pl.pallas_call(hand_out, out_shape=(air, air, plate, plate, plate), in_sp...]
where the time goes in v2:
time: 29.7 us; the launch traced here: 29.5 us
  Pallas kernels  28.9 us (97%)
  between operations  0.65 us (2%)
    pallas_call x1, Pallas kernels, on_device(): pl.pallas_call(functools.partial(kernel, counts), out_shape=(air, air, pl...  27 us
    pallas_call x1, Pallas kernels, on_device(): pl.pallas_call(hand_out, out_shape=(air, air, plate, plate, plate), in_sp...  1.89 us

profile of v2, /device:TPU:0, one launch (start us, length us, event | category | flops | bytes accessed | tf_op | source)
XLA Modules:
  0.0 29.5 jit_solution(5456133469952068571)
XLA Ops:
  0.6 27.0 %shard_map.173 = (f32[16,32,128]{2,1,0:T(8,128)}, f32[16,32,128]{2,1,0:T(8,128)}, f32[16,32]{1,0:T(8,128)}, f32[16,32]{1,0:T(8,128)}, f32[16,32]{1,0:T(8,128)}) custom-call(f32[16,32,128]{2,1,0:T(8,128)} %refs_0_.1, f32[16,32,128]{2,1,0:T(8,128)} %refs_1_.1, f32[16,32]{1,0:T(8,128)} %refs_2_.1, f32[16,32]{1,0:T(8,128)} %refs_3_.1, f32[16,32,128]{2,1,0:T(8,128)} %refs_4_.1, ...), custom_call_target="tpu_custom_call" | custom-call | flops 15728640 | bytes 1835008 | tf_op jit(solution)/shard_map/pallas_call | solution.py:457
  27.6 1.9 %shard_map.174 = (f32[16,32,128]{2,1,0:T(8,128)}, f32[16,32,128]{2,1,0:T(8,128)}, f32[16,32]{1,0:T(8,128)}, f32[16,32]{1,0:T(8,128)}, f32[16,32]{1,0:T(8,128)}) custom-call(f32[16,32,128]{2,1,0:T(8,128)} %get-tuple-element.10.refs_0_, f32[16,32,128]{2,1,0:T(8,128)} %get-tuple-element.11.refs_1_, f32[16,32]{1,0:T(8,128)} %get-tuple-element.12.refs_2_, ...), custom_call_target="tpu_custom_call" | custom-call | tf_op jit(solution)/shard_map/pallas_call | solution.py:474
